TPU v7x, 512 devices: a whole 4x4x16 slice. The times are simulated.
512 devices in a mesh: ctx: 64 (over z, x_lo, core), head: 8 (over y, x_hi).
Axes of the slice: x: 4 (x_hi: 2, x_lo: 2; x = x_hi * 2 + x_lo), y: 4, z: 16, core: 2. Of those that a mesh axis runs over, the one named last changes fastest.
Arguments:
- queries: bfloat16 [16384, 8192], P(('ctx', 'head')), may hold values from -8 to 8
- kv_cache: bfloat16 [2, 131072, 1024], P(None, 'ctx', 'head'), may hold values from -8 to 8
- anchor_src: int32 [64], P('ctx'), may hold values from 0 to 63, as said below
- stretch_pos: int32 [64], P('ctx'), may hold values from 0 to 1792, as said below
Outputs:
- attended: bfloat16 [16384, 8192], P(('ctx', 'head'))
Inputs may be any that keep to these rules, and one draw needn't show every extreme that they name: Documents are runs of whole blocks: anchor_src[b] is the first block of block b's document, never after b, the same for all blocks of one document, anchor_src[0] = 0; a document covers 1 to 8 blocks and some document covers exactly 8 blocks. `stretch_pos`: A multiple of 256; some block has the largest value and some block has 0.
All inputs are finite; a program needn't handle non-finite values.
Results may differ from a plain program's by a relative error of at most 0.0055.
Values may be sent and summed in bfloat16 or wider, within the bound.
No kernel may reach another device: no remote copies, remote signals or barrier semaphores. Data moves between devices by JAX's collectives and lax.ppermute only.
A program may use at most 64 MiB of HBM per device.

v0:
```python
import functools
import math

import jax
import jax.numpy as jnp
from jax import lax
from jax.experimental import pallas as pl
from jax.experimental.pallas import tpu as pltpu
from jax.sharding import PartitionSpec as P

QUERY_HEAD_COUNT = 64
KEY_HEADS = 8
HEAD_SIZE = 128
GROUP = QUERY_HEAD_COUNT // KEY_HEADS
BLOCK_QUERIES = 256
CACHE_SLOTS = 2048
ANCHOR_SLOTS = 512
SPAN = 8
TILE = 256
STACK = 2
LOCAL_TILES = CACHE_SLOTS // TILE
ANCHOR_TILES = ANCHOR_SLOTS // TILE

masked_score = -1e30
EXP2_SCALE = math.log2(math.e) / math.sqrt(HEAD_SIZE)
SAFE_LOW, SAFE_HIGH = 2.0**-60, 2.0**60


def head_columns(g):
    return slice(g * HEAD_SIZE, (g + 1) * HEAD_SIZE)


def cut_kernel(queries, outgoing):
    pieces, _, width = outgoing.shape
    for h in range(pieces):
        outgoing[h] = queries[:, h * width:(h + 1) * width]


def choose_kernel(shift, scalars, moved, held, after, out):
    arrived = (scalars[1] & shift) != 0

    @pl.when(arrived)
    def _():
        out[...] = moved[...]

    @pl.when(jnp.logical_not(arrived))
    def _():
        out[...] = held[...]


def widen_kernel(part_ref, after, keys, vals):
    widen_into(part_ref, keys, vals)


def widen_into(part_ref, keys, vals):
    keys[...] = part_ref[0].astype(jnp.float32).T.astype(jnp.bfloat16)
    vals[:, 0:HEAD_SIZE] = part_ref[1]
    vals[:, HEAD_SIZE:] = jnp.ones(part_ref.shape[1:], jnp.bfloat16)


def scaled_scores(q, keys):
    return jnp.dot(q, keys, preferred_element_type=jnp.float32) * EXP2_SCALE


def is_safe(low, high):
    return jnp.logical_and(jnp.min(low) > SAFE_LOW, jnp.max(high) < SAFE_HIGH).astype(jnp.int32)


def stacked(q_ref, first):
    return jnp.concatenate([q_ref[:, head_columns(first + g)] for g in range(STACK)], axis=0)


def rows_of(g):
    return slice(g * BLOCK_QUERIES, (g + 1) * BLOCK_QUERIES)


def local_kernel(scalars, q_ref, keys, vals, state_ref, peak_ref, safe_ref, scores, weights):
    heads = state_ref.shape[0]
    full_tiles = scalars[0]
    row = lax.broadcasted_iota(jnp.int32, (BLOCK_QUERIES, TILE), 0)
    col = lax.broadcasted_iota(jnp.int32, (BLOCK_QUERIES, TILE), 1)
    slant = col - row

    def tile_of(tile):
        return slice(tile * TILE, (tile + 1) * TILE)

    def unshifted(tiles, masked):
        span = tiles * TILE

        def weigh(stack):
            q = stacked(q_ref, stack * STACK)
            for tile in range(tiles):
                s = scaled_scores(q, keys[:, tile_of(tile)])
                if tile >= masked:
                    allowed = slant <= (full_tiles - tile) * TILE
                    s = jnp.where(jnp.concatenate([allowed] * STACK, axis=0), s, masked_score)
                weights[stack % 2, :, tile_of(tile)] = jnp.exp2(s).astype(jnp.bfloat16)

        low = high = None
        weigh(0)
        for stack in range(heads // STACK):
            if (stack + 1) * STACK < heads:
                weigh(stack + 1)
            mixed = jnp.dot(weights[stack % 2, :, 0:span], vals[0:span, :], preferred_element_type=jnp.float32)
            for g in range(STACK):
                state_ref[stack * STACK + g] = mixed[rows_of(g)]
            total = mixed[:, HEAD_SIZE:]
            low = total if low is None else jnp.minimum(low, total)
            high = total if high is None else jnp.maximum(high, total)
        safe_ref[0] = is_safe(low, high)

    @pl.when(full_tiles == LOCAL_TILES - 1)
    def _():
        unshifted(LOCAL_TILES, LOCAL_TILES - 1)

    @pl.when(full_tiles < LOCAL_TILES - 1)
    def _():
        unshifted(LOCAL_TILES - 1, 0)

    @pl.when(safe_ref[0] == 0)
    def _():
        def tile_at(tile):
            return pl.ds(pl.multiple_of(tile * TILE, TILE), TILE)

        for g in range(heads):
            q = q_ref[:, head_columns(g)]

            def score_tile(tile, peak):
                s = scaled_scores(q, keys[:, tile_at(tile)])
                s = jnp.where(slant <= (full_tiles - tile) * TILE, s, masked_score)
                scores[:, tile_at(tile)] = s
                return jnp.maximum(peak, jnp.max(s, axis=1, keepdims=True))

            peak = lax.fori_loop(0, full_tiles + 1, score_tile,
                                 jnp.full((BLOCK_QUERIES, 1), masked_score, jnp.float32))

            def mix_tile(tile, mixed):
                p = jnp.exp2(scores[:, tile_at(tile)] - peak).astype(jnp.bfloat16)
                return mixed + jnp.dot(p, vals[tile_at(tile), :], preferred_element_type=jnp.float32)

            state_ref[g] = lax.fori_loop(0, full_tiles + 1, mix_tile,
                                         jnp.zeros((BLOCK_QUERIES, 2 * HEAD_SIZE), jnp.float32))
            peak_ref[g] = jnp.broadcast_to(peak, peak_ref.shape[1:])


def anchor_kernel(scalars, safe, moved, held, q_ref, states, peaks, out_ref, anchor, keys, vals, weights, safe_ref):
    heads = states.shape[0]
    has_anchor = scalars[1] > 0
    choose_kernel(1, scalars, moved, held, None, anchor)
    widen_into(anchor, keys, vals)

    def score(q):
        return jnp.where(has_anchor, scaled_scores(q, keys[...]), masked_score)

    def write(g, top, bottom):
        out_ref[:, head_columns(g)] = (top / bottom).astype(jnp.bfloat16)

    for stack in range(heads // STACK):
        weights[stack] = jnp.exp2(score(stacked(q_ref, stack * STACK))).astype(jnp.bfloat16)
    high = None
    for stack in range(heads // STACK):
        both = jnp.dot(weights[stack], vals[...], preferred_element_type=jnp.float32)
        for g in range(STACK):
            mixed = both[rows_of(g)] + states[stack * STACK + g]
            total = mixed[:, HEAD_SIZE:]
            write(stack * STACK + g, mixed[:, :HEAD_SIZE], total)
            high = total if high is None else jnp.maximum(high, total)
    safe_ref[0] = is_safe(jnp.ones_like(high), high) * safe[0]

    @pl.when(safe_ref[0] == 0)
    def _():
        for g in range(heads):
            s = score(q_ref[:, head_columns(g)])
            old = jnp.where(safe[0] == 1, 0.0, peaks[g])
            peak = jnp.maximum(jnp.max(s, axis=1, keepdims=True), old)
            for at in range(0, ANCHOR_SLOTS, HEAD_SIZE):
                p = jnp.exp2(s[:, at:at + HEAD_SIZE] - peak)
                weights[0, 0:BLOCK_QUERIES, at:at + HEAD_SIZE] = p.astype(jnp.bfloat16)
            mixed = jnp.dot(weights[0, 0:BLOCK_QUERIES], vals[...], preferred_element_type=jnp.float32)
            factor = jnp.exp2(old - peak)
            write(g, mixed[:, :HEAD_SIZE] + states[g, :, :HEAD_SIZE] * factor,
                  mixed[:, HEAD_SIZE:] + states[g, :, HEAD_SIZE:] * factor)


def cost(heads, keys):
    flops = 4 * BLOCK_QUERIES * heads * keys * HEAD_SIZE
    return pl.CostEstimate(flops=flops, bytes_accessed=2 * 2**20, transcendentals=flops // 512)


smem = pl.BlockSpec(memory_space=pltpu.SMEM)
vmem = pl.BlockSpec(memory_space=pltpu.VMEM)
anywhere = pl.BlockSpec(memory_space=pl.ANY)
small = pltpu.CompilerParams(vmem_limit_bytes=4 * 2**20)
params = pltpu.CompilerParams(vmem_limit_bytes=24 * 2**20)
slight = pl.CostEstimate(flops=1000, bytes_accessed=1000, transcendentals=0)
safe_flag = jax.ShapeDtypeStruct((1,), jnp.int32)


def wide_shapes(count):
    return (jax.ShapeDtypeStruct((HEAD_SIZE, count), jnp.bfloat16),
            jax.ShapeDtypeStruct((count, 2 * HEAD_SIZE), jnp.bfloat16))


def cut(queries):
    rows, width = queries.shape
    return pl.pallas_call(
        cut_kernel,
        out_shape=jax.ShapeDtypeStruct((KEY_HEADS, rows, width // KEY_HEADS), jnp.bfloat16),
        in_specs=[vmem],
        out_specs=vmem,
        compiler_params=small,
        cost_estimate=slight,
        name="cut",
    )(queries)


def choose(shift, scalars, moved, held, after):
    return pl.pallas_call(
        functools.partial(choose_kernel, shift),
        out_shape=jax.ShapeDtypeStruct(held.shape, held.dtype),
        in_specs=[smem, vmem, vmem, anywhere],
        out_specs=vmem,
        compiler_params=small,
        cost_estimate=slight,
        name="choose",
    )(scalars, moved, held, after)


def widen(kv, after):
    return pl.pallas_call(
        widen_kernel,
        out_shape=wide_shapes(CACHE_SLOTS),
        in_specs=[vmem, anywhere],
        out_specs=(vmem, vmem),
        compiler_params=params,
        cost_estimate=cost(GROUP, CACHE_SLOTS),
        name="widen",
    )(kv, after)


def attend_local(scalars, q, keys, vals):
    return pl.pallas_call(
        local_kernel,
        out_shape=(
            jax.ShapeDtypeStruct((GROUP, BLOCK_QUERIES, 2 * HEAD_SIZE), jnp.float32),
            jax.ShapeDtypeStruct((GROUP, BLOCK_QUERIES, HEAD_SIZE), jnp.float32),
            safe_flag,
        ),
        in_specs=[smem, vmem, vmem, vmem],
        out_specs=(vmem, vmem, smem),
        scratch_shapes=[
            pltpu.VMEM((BLOCK_QUERIES, CACHE_SLOTS), jnp.float32),
            pltpu.VMEM((2, STACK * BLOCK_QUERIES, CACHE_SLOTS), jnp.bfloat16),
        ],
        compiler_params=params,
        cost_estimate=cost(GROUP, CACHE_SLOTS),
        name="attend_local",
    )(scalars, q, keys, vals)


def attend_anchor(scalars, moved, held, q, states, peaks, safe):
    return pl.pallas_call(
        anchor_kernel,
        out_shape=jax.ShapeDtypeStruct(q.shape, jnp.bfloat16),
        in_specs=[smem] * 2 + [vmem] * 5,
        out_specs=vmem,
        scratch_shapes=[
            pltpu.VMEM(held.shape, held.dtype),
            *(pltpu.VMEM(wide.shape, wide.dtype) for wide in wide_shapes(ANCHOR_SLOTS)),
            pltpu.VMEM((GROUP // STACK, STACK * BLOCK_QUERIES, ANCHOR_SLOTS), jnp.bfloat16),
            pltpu.SMEM((1,), jnp.int32),
        ],
        compiler_params=params,
        cost_estimate=cost(GROUP, ANCHOR_SLOTS),
        name="attend_anchor",
    )(scalars, safe, moved, held, q, states, peaks)


def body(queries, kv_cache, anchor_src, stretch_pos):
    block = lax.axis_index("ctx").astype(jnp.int32)
    blocks = lax.axis_size("ctx")
    scalars = jnp.stack([stretch_pos[0] // TILE, block - anchor_src[0]])
    held, outgoing = lax.optimization_barrier((kv_cache[:, :ANCHOR_SLOTS, :], cut(queries)))

    def from_earlier(held, shift):
        return lax.ppermute(held, "ctx", [(b, b + shift) for b in range(blocks - shift)])

    moved = from_earlier(held, 4)
    q = lax.all_to_all(outgoing, "head", split_axis=0, concat_axis=0, tiled=True)
    q = q.reshape(BLOCK_QUERIES, GROUP * HEAD_SIZE)
    held = choose(4, scalars, moved, held, scalars)
    moved = from_earlier(held, 2)
    keys, vals = widen(kv_cache, q)
    held = choose(2, scalars, moved, held, keys)
    moved = from_earlier(held, 1)
    state = attend_local(scalars, q, keys, vals)
    result = attend_anchor(scalars, moved, held, q, *state)
    return lax.all_to_all(result, "head", split_axis=0, concat_axis=1, tiled=True)


def solution(mesh):
    in_specs = (P(("ctx", "head"), None), P(None, "ctx", "head"), P("ctx"), P("ctx"))
    out_specs = P(("ctx", "head"), None)
    return jax.shard_map(body, mesh=mesh, in_specs=in_specs, out_specs=out_specs, check_vma=False)
```

profile of v0, /device:TPU:227, one launch (start us, length us, event | category | flops | bytes accessed | tf_op | source)
XLA Modules:
  0.0 94.9 jit_solution(7605176454039952057)
XLA Ops:
  0.0 1.0 %slice.3.held = bf16[2,512,128]{2,1,0:T(8,128)(2,1)S(1)} slice(bf16[2,2048,128]{2,1,0:T(8,128)(2,1)} %part_ref.1), slice={[0:2], [0:512], [0:128]} | slice | bytes 524288 | tf_op jit(solution)/shard_map/slice | solution.py:283
  1.0 0.0 copy-start
  1.0 1.0 %copy-done = bf16[32,8192]{1,0:T(8,128)(2,1)S(1)} copy-done((bf16[32,8192]{1,0:T(8,128)(2,1)S(1)}, bf16[32,8192]{1,0:T(8,128)(2,1)}, u32[]{:S(2)}) %copy-start) | copy-done | bytes 524312
  2.0 0.0 copy-start.1
  2.0 0.8 cut.1
  2.8 5.8 %all-to-all-start = ((bf16[8,32,1024]{2,1,0:T(8,128)(2,1)}), bf16[8,32,1024]{2,1,0:T(8,128)(2,1)S(1)}, u32[]{:S(2)}, u32[]{:S(2)}) async-start(bf16[8,32,1024]{2,1,0:T(8,128)(2,1)} %cut.1), calls=%async_computation | async-start | bytes 1048576 | tf_op jit(solution)/shard_map/all_to_all | solution.py:289
  8.6 4.7 %collective-permute-start = (bf16[2,512,128]{2,1,0:T(8,128)(2,1)S(1)}, bf16[2,512,128]{2,1,0:T(8,128)(2,1)S(1)}, u32[]{:S(2)}, u32[]{:S(2)}) collective-permute-start(bf16[2,512,128]{2,1,0:T(8,128)(2,1)S(1)} %slice.3.held), channel_id=1, source_target_pairs={{0,32},{8,40},{16,48},{24,56},{32,64},{40,72},{48,80},{56,88},{64,... | collective-permute-start | bytes 786440 | tf_op jit(solution)/shard_map/ppermute | solution.py:286
  14.7 0.1 pad_add_fusion.scalars.after
  14.7 3.2 %collective-permute-done.moved = bf16[2,512,128]{2,1,0:T(8,128)(2,1)S(1)} collective-permute-done((bf16[2,512,128]{2,1,0:T(8,128)(2,1)S(1)}, bf16[2,512,128]{2,1,0:T(8,128)(2,1)S(1)}, u32[]{:S(2)}, u32[]{:S(2)}) %collective-permute-start) | collective-permute-done | bytes 262176 | tf_op jit(solution)/shard_map/ppermute | solution.py:286
  18.0 0.6 choose.2.held
  18.6 6.2 %collective-permute-start.1 = (bf16[2,512,128]{2,1,0:T(8,128)(2,1)S(1)}, bf16[2,512,128]{2,1,0:T(8,128)(2,1)S(1)}, u32[]{:S(2)}, u32[]{:S(2)}) collective-permute-start(bf16[2,512,128]{2,1,0:T(8,128)(2,1)S(1)} %choose.2.held), channel_id=1, source_target_pairs={{0,16},{8,24},{16,32},{24,40},{32,48},{40,56},{48,64},{56,72},{64,... | collective-permute-start | bytes 786440 | tf_op jit(solution)/shard_map/ppermute | solution.py:286
  24.8 0.0 all-to-all-done
  24.8 0.0 copy-done.1
  24.8 0.3 widen.1
  25.1 3.4 %collective-permute-done.1.moved = bf16[2,512,128]{2,1,0:T(8,128)(2,1)S(1)} collective-permute-done((bf16[2,512,128]{2,1,0:T(8,128)(2,1)S(1)}, bf16[2,512,128]{2,1,0:T(8,128)(2,1)S(1)}, u32[]{:S(2)}, u32[]{:S(2)}) %collective-permute-start.1) | collective-permute-done | bytes 262176 | tf_op jit(solution)/shard_map/ppermute | solution.py:286
  28.5 0.6 choose.3.held
  29.0 8.9 %collective-permute-start.2 = (bf16[2,512,128]{2,1,0:T(8,128)(2,1)S(1)}, bf16[2,512,128]{2,1,0:T(8,128)(2,1)S(1)}, u32[]{:S(2)}, u32[]{:S(2)}) collective-permute-start(bf16[2,512,128]{2,1,0:T(8,128)(2,1)S(1)} %choose.3.held), channel_id=1, source_target_pairs={{0,8},{8,16},{16,24},{24,32},{32,40},{40,48},{48,56},{56,64},{64,7... | collective-permute-start | bytes 786440 | tf_op jit(solution)/shard_map/ppermute | solution.py:286
  37.9 36.4 %attend_local.1 = (f32[8,256,256]{2,1,0:T(8,128)S(1)}, f32[8,256,128]{2,1,0:T(8,128)S(1)}, s32[1]{0:T(128)}) custom-call(s32[2]{0:T(128)S(1)} %pad_add_fusion.scalars.after, bf16[256,1024]{1,0:T(8,128)(2,1)S(1)} %bitcast.15, bf16[128,2048]{1,0:T(8,128)(2,1)S(1)} %get-tuple-element.13.keys.after, bf16[2048,256]{1,0:T(8,128)(2,1)S(1)} %get-tuple-element.14.vals), custom_call_target="tpu_custom_call" | custom-call | flops 2147483648 | bytes 2097152 | tf_op jit(solution)/shard_map/attend_local/pallas_call | solution.py:242
  74.4 0.0 collective-permute-done.2.moved
  74.4 5.1 %attend_anchor.1 = bf16[256,1024]{1,0:T(8,128)(2,1)S(1)} custom-call(s32[2]{0:T(128)S(1)} %pad_add_fusion.scalars.after, s32[1]{0:T(128)} %get-tuple-element.15.safe, bf16[2,512,128]{2,1,0:T(8,128)(2,1)S(1)} %collective-permute-done.2.moved, bf16[2,512,128]{2,1,0:T(8,128)(2,1)S(1)} %choose.3.held, bf16[256,1024]{1,0:T(8,128)(2,1)S(1)} %bitcast.16, ...), custom_call_target="tpu_custom_call" | custom-call | flops 536870912 | bytes 2097152 | tf_op jit(solution)/shard_map/attend_anchor/pallas_call | solution.py:262
  79.5 14.6 %all_to_all.24 = bf16[8,32,1024]{2,1,0:T(8,128)(2,1)S(1)} all-to-all(bf16[8,32,1024]{2,1,0:T(8,128)(2,1)S(1)} %bitcast.17), channel_id=1, replica_groups=mesh['ctx'=64,'head'=8] {'head'}, dimensions={0} | all-to-all | bytes 1048576 | tf_op jit(solution)/shard_map/all_to_all | solution.py:298
  94.1 0.8 copy.6
Async XLA Ops:
  1.0 1.0 %copy-start = (bf16[32,8192]{1,0:T(8,128)(2,1)S(1)}, bf16[32,8192]{1,0:T(8,128)(2,1)}, u32[]{:S(2)}) copy-start(bf16[32,8192]{1,0:T(8,128)(2,1)} %queries.1) | copy-start | bytes 1572868
  2.0 22.8 %copy-start.1 = (bf16[2,2048,128]{2,1,0:T(8,128)(2,1)S(1)}, bf16[2,2048,128]{2,1,0:T(8,128)(2,1)}, u32[]{:S(2)}) copy-start(bf16[2,2048,128]{2,1,0:T(8,128)(2,1)} %part_ref.1) | copy-start | bytes 3145732
  2.8 21.9 %all-to-all-start = ((bf16[8,32,1024]{2,1,0:T(8,128)(2,1)}), bf16[8,32,1024]{2,1,0:T(8,128)(2,1)S(1)}, u32[]{:S(2)}, u32[]{:S(2)}) async-start(bf16[8,32,1024]{2,1,0:T(8,128)(2,1)} %cut.1), calls=%async_computation | async-start | bytes 1048576 | tf_op jit(solution)/shard_map/all_to_all | solution.py:289
  8.6 9.4 %collective-permute-start = (bf16[2,512,128]{2,1,0:T(8,128)(2,1)S(1)}, bf16[2,512,128]{2,1,0:T(8,128)(2,1)S(1)}, u32[]{:S(2)}, u32[]{:S(2)}) collective-permute-start(bf16[2,512,128]{2,1,0:T(8,128)(2,1)S(1)} %slice.3.held), channel_id=1, source_target_pairs={{0,32},{8,40},{16,48},{24,56},{32,64},{40,72},{48,80},{56,88},{64,... | collective-permute-start | bytes 786440 | tf_op jit(solution)/shard_map/ppermute | solution.py:286
  18.6 9.9 %collective-permute-start.1 = (bf16[2,512,128]{2,1,0:T(8,128)(2,1)S(1)}, bf16[2,512,128]{2,1,0:T(8,128)(2,1)S(1)}, u32[]{:S(2)}, u32[]{:S(2)}) collective-permute-start(bf16[2,512,128]{2,1,0:T(8,128)(2,1)S(1)} %choose.2.held), channel_id=1, source_target_pairs={{0,16},{8,24},{16,32},{24,40},{32,48},{40,56},{48,64},{56,72},{64,... | collective-permute-start | bytes 786440 | tf_op jit(solution)/shard_map/ppermute | solution.py:286
  29.0 45.3 %collective-permute-start.2 = (bf16[2,512,128]{2,1,0:T(8,128)(2,1)S(1)}, bf16[2,512,128]{2,1,0:T(8,128)(2,1)S(1)}, u32[]{:S(2)}, u32[]{:S(2)}) collective-permute-start(bf16[2,512,128]{2,1,0:T(8,128)(2,1)S(1)} %choose.3.held), channel_id=1, source_target_pairs={{0,8},{8,16},{16,24},{24,32},{32,40},{40,48},{48,56},{56,64},{64,7... | collective-permute-start | bytes 786440 | tf_op jit(solution)/shard_map/ppermute | solution.py:286
where the time goes:
time: 95.3 us; the launch traced here: 94.9 us
  Pallas kernels  43.8 us (46%)
  starting transfers between devices  25.6 us (27%)
  blocking collectives  14.6 us (15%)
  waiting for transfers between devices  6.64 us (7%)
  local copies, waits for them, and re-layouts  2.84 us (3%)
  between operations  1.42 us (1%)
    pallas_call x1, Pallas kernels, attend_local(): pl.pallas_call(local_kernel, out_shape=(jax.ShapeDtypeStruct((GROUP, BLOC...  36.4 us
    ppermute x3, starting transfers between devices, from_earlier(): lax.ppermute(held, 'ctx', [(b, b + shift) for b in range(blocks - shift)])  19.8 us
    all_to_all x1, blocking collectives, body(): lax.all_to_all(result, 'head', split_axis=0, concat_axis=1, tiled=True)  14.6 us
    ppermute x3, waiting for transfers between devices, from_earlier(): lax.ppermute(held, 'ctx', [(b, b + shift) for b in range(blocks - shift)])  6.63 us
    all_to_all x1, starting transfers between devices, body(): lax.all_to_all(outgoing, 'head', split_axis=0, concat_axis=0, tiled=True)  5.75 us
    pallas_call x1, Pallas kernels, attend_anchor(): pl.pallas_call(anchor_kernel, out_shape=jax.ShapeDtypeStruct(q.shape, jnp...  5.13 us
  transfers between devices with their start and end apart: 4, of which 2 were waited for; matrix products, arithmetic and copies ran while one was open for 0% of the time, Pallas kernels for 39%

commit v1 on v0

--- a/solution.py
+++ b/solution.py
@@ -17,9 +17,7 @@
 ANCHOR_SLOTS = 512
 SPAN = 8
 TILE = 256
-STACK = 2
-LOCAL_TILES = CACHE_SLOTS // TILE
-ANCHOR_TILES = ANCHOR_SLOTS // TILE
+CHUNK = 512
 
 masked_score = -1e30
 EXP2_SCALE = math.log2(math.e) / math.sqrt(HEAD_SIZE)
@@ -30,7 +28,7 @@
     return slice(g * HEAD_SIZE, (g + 1) * HEAD_SIZE)
 
 
-def cut_kernel(queries, outgoing):
+def cut_kernel(queries, after, outgoing):
     pieces, _, width = outgoing.shape
     for h in range(pieces):
         outgoing[h] = queries[:, h * width:(h + 1) * width]
@@ -66,56 +64,42 @@
     return jnp.logical_and(jnp.min(low) > SAFE_LOW, jnp.max(high) < SAFE_HIGH).astype(jnp.int32)
 
 
-def stacked(q_ref, first):
-    return jnp.concatenate([q_ref[:, head_columns(first + g)] for g in range(STACK)], axis=0)
-
-
-def rows_of(g):
-    return slice(g * BLOCK_QUERIES, (g + 1) * BLOCK_QUERIES)
+def sum_in_parts(weights, vals, span, parts=2):
+    step = span // parts
+    products = [
+        jnp.dot(weights[:, i:i + step], vals[i:i + step, :], preferred_element_type=jnp.float32)
+        for i in range(0, span, step)
+    ]
+    return functools.reduce(jnp.add, products)
 
 
 def local_kernel(scalars, q_ref, keys, vals, state_ref, peak_ref, safe_ref, scores, weights):
     heads = state_ref.shape[0]
     full_tiles = scalars[0]
-    row = lax.broadcasted_iota(jnp.int32, (BLOCK_QUERIES, TILE), 0)
-    col = lax.broadcasted_iota(jnp.int32, (BLOCK_QUERIES, TILE), 1)
+    row = lax.broadcasted_iota(jnp.int32, (BLOCK_QUERIES, CHUNK), 0)
+    col = lax.broadcasted_iota(jnp.int32, (BLOCK_QUERIES, CHUNK), 1)
     slant = col - row
 
-    def tile_of(tile):
-        return slice(tile * TILE, (tile + 1) * TILE)
-
-    def unshifted(tiles, masked):
-        span = tiles * TILE
-
-        def weigh(stack):
-            q = stacked(q_ref, stack * STACK)
-            for tile in range(tiles):
-                s = scaled_scores(q, keys[:, tile_of(tile)])
-                if tile >= masked:
-                    allowed = slant <= (full_tiles - tile) * TILE
-                    s = jnp.where(jnp.concatenate([allowed] * STACK, axis=0), s, masked_score)
-                weights[stack % 2, :, tile_of(tile)] = jnp.exp2(s).astype(jnp.bfloat16)
-
-        low = high = None
-        weigh(0)
-        for stack in range(heads // STACK):
-            if (stack + 1) * STACK < heads:
-                weigh(stack + 1)
-            mixed = jnp.dot(weights[stack % 2, :, 0:span], vals[0:span, :], preferred_element_type=jnp.float32)
-            for g in range(STACK):
-                state_ref[stack * STACK + g] = mixed[rows_of(g)]
-            total = mixed[:, HEAD_SIZE:]
-            low = total if low is None else jnp.minimum(low, total)
-            high = total if high is None else jnp.maximum(high, total)
-        safe_ref[0] = is_safe(low, high)
-
-    @pl.when(full_tiles == LOCAL_TILES - 1)
-    def _():
-        unshifted(LOCAL_TILES, LOCAL_TILES - 1)
-
-    @pl.when(full_tiles < LOCAL_TILES - 1)
-    def _():
-        unshifted(LOCAL_TILES - 1, 0)
+    def weigh(g, chunks):
+        q = q_ref[:, head_columns(g)]
+        for chunk in range(chunks):
+            at = slice(chunk * CHUNK, (chunk + 1) * CHUNK)
+            s = scaled_scores(q, keys[:, at])
+            if chunk == chunks - 1:
+                s = jnp.where(slant <= full_tiles * TILE - chunk * CHUNK, s, masked_score)
+            weights[g % 2, :, at] = jnp.exp2(s).astype(jnp.bfloat16)
+
+    def unshifted(chunks):
+        weigh(0, chunks)
+        for g in range(heads):
+            if g + 1 < heads:
+                weigh(g + 1, chunks)
+            state_ref[g] = sum_in_parts(weights.at[g % 2], vals, chunks * CHUNK)
+
+    for chunks in range(1, CACHE_SLOTS // CHUNK + 1):
+        pl.when(full_tiles * TILE // CHUNK == chunks - 1)(functools.partial(unshifted, chunks))
+    totals = [state_ref[g, :, HEAD_SIZE:] for g in range(heads)]
+    safe_ref[0] = is_safe(functools.reduce(jnp.minimum, totals), functools.reduce(jnp.maximum, totals))
 
     @pl.when(safe_ref[0] == 0)
     def _():
@@ -127,7 +111,7 @@
 
             def score_tile(tile, peak):
                 s = scaled_scores(q, keys[:, tile_at(tile)])
-                s = jnp.where(slant <= (full_tiles - tile) * TILE, s, masked_score)
+                s = jnp.where(slant[:, :TILE] <= (full_tiles - tile) * TILE, s, masked_score)
                 scores[:, tile_at(tile)] = s
                 return jnp.maximum(peak, jnp.max(s, axis=1, keepdims=True))
 
@@ -155,16 +139,14 @@
     def write(g, top, bottom):
         out_ref[:, head_columns(g)] = (top / bottom).astype(jnp.bfloat16)
 
-    for stack in range(heads // STACK):
-        weights[stack] = jnp.exp2(score(stacked(q_ref, stack * STACK))).astype(jnp.bfloat16)
+    for g in range(heads):
+        weights[g] = jnp.exp2(score(q_ref[:, head_columns(g)])).astype(jnp.bfloat16)
     high = None
-    for stack in range(heads // STACK):
-        both = jnp.dot(weights[stack], vals[...], preferred_element_type=jnp.float32)
-        for g in range(STACK):
-            mixed = both[rows_of(g)] + states[stack * STACK + g]
-            total = mixed[:, HEAD_SIZE:]
-            write(stack * STACK + g, mixed[:, :HEAD_SIZE], total)
-            high = total if high is None else jnp.maximum(high, total)
+    for g in range(heads):
+        mixed = sum_in_parts(weights.at[g], vals, ANCHOR_SLOTS) + states[g]
+        total = mixed[:, HEAD_SIZE:]
+        write(g, mixed[:, :HEAD_SIZE], total)
+        high = total if high is None else jnp.maximum(high, total)
     safe_ref[0] = is_safe(jnp.ones_like(high), high) * safe[0]
 
     @pl.when(safe_ref[0] == 0)
@@ -175,8 +157,8 @@
             peak = jnp.maximum(jnp.max(s, axis=1, keepdims=True), old)
             for at in range(0, ANCHOR_SLOTS, HEAD_SIZE):
                 p = jnp.exp2(s[:, at:at + HEAD_SIZE] - peak)
-                weights[0, 0:BLOCK_QUERIES, at:at + HEAD_SIZE] = p.astype(jnp.bfloat16)
-            mixed = jnp.dot(weights[0, 0:BLOCK_QUERIES], vals[...], preferred_element_type=jnp.float32)
+                weights[g, :, at:at + HEAD_SIZE] = p.astype(jnp.bfloat16)
+            mixed = jnp.dot(weights[g], vals[...], preferred_element_type=jnp.float32)
             factor = jnp.exp2(old - peak)
             write(g, mixed[:, :HEAD_SIZE] + states[g, :, :HEAD_SIZE] * factor,
                   mixed[:, HEAD_SIZE:] + states[g, :, HEAD_SIZE:] * factor)
@@ -201,27 +183,27 @@
             jax.ShapeDtypeStruct((count, 2 * HEAD_SIZE), jnp.bfloat16))
 
 
-def cut(queries):
+def cut(queries, after):
     rows, width = queries.shape
     return pl.pallas_call(
         cut_kernel,
         out_shape=jax.ShapeDtypeStruct((KEY_HEADS, rows, width // KEY_HEADS), jnp.bfloat16),
-        in_specs=[vmem],
+        in_specs=[vmem, anywhere],
         out_specs=vmem,
         compiler_params=small,
         cost_estimate=slight,
         name="cut",
-    )(queries)
-
-
-def choose(shift, scalars, moved, held, after):
+    )(queries, after)
+
+
+def choose(shift, scalars, moved, held, after, estimate):
     return pl.pallas_call(
         functools.partial(choose_kernel, shift),
         out_shape=jax.ShapeDtypeStruct(held.shape, held.dtype),
         in_specs=[smem, vmem, vmem, anywhere],
         out_specs=vmem,
         compiler_params=small,
-        cost_estimate=slight,
+        cost_estimate=estimate,
         name="choose",
     )(scalars, moved, held, after)
 
@@ -250,7 +232,7 @@
         out_specs=(vmem, vmem, smem),
         scratch_shapes=[
             pltpu.VMEM((BLOCK_QUERIES, CACHE_SLOTS), jnp.float32),
-            pltpu.VMEM((2, STACK * BLOCK_QUERIES, CACHE_SLOTS), jnp.bfloat16),
+            pltpu.VMEM((2, BLOCK_QUERIES, CACHE_SLOTS), jnp.bfloat16),
         ],
         compiler_params=params,
         cost_estimate=cost(GROUP, CACHE_SLOTS),
@@ -267,7 +249,7 @@
         scratch_shapes=[
             pltpu.VMEM(held.shape, held.dtype),
             *(pltpu.VMEM(wide.shape, wide.dtype) for wide in wide_shapes(ANCHOR_SLOTS)),
-            pltpu.VMEM((GROUP // STACK, STACK * BLOCK_QUERIES, ANCHOR_SLOTS), jnp.bfloat16),
+            pltpu.VMEM((GROUP, BLOCK_QUERIES, ANCHOR_SLOTS), jnp.bfloat16),
             pltpu.SMEM((1,), jnp.int32),
         ],
         compiler_params=params,
@@ -280,18 +262,18 @@
     block = lax.axis_index("ctx").astype(jnp.int32)
     blocks = lax.axis_size("ctx")
     scalars = jnp.stack([stretch_pos[0] // TILE, block - anchor_src[0]])
-    held, outgoing = lax.optimization_barrier((kv_cache[:, :ANCHOR_SLOTS, :], cut(queries)))
+    held = lax.optimization_barrier(kv_cache[:, :ANCHOR_SLOTS, :])
 
     def from_earlier(held, shift):
         return lax.ppermute(held, "ctx", [(b, b + shift) for b in range(blocks - shift)])
 
     moved = from_earlier(held, 4)
-    q = lax.all_to_all(outgoing, "head", split_axis=0, concat_axis=0, tiled=True)
+    q = lax.all_to_all(cut(queries, held), "head", split_axis=0, concat_axis=0, tiled=True)
     q = q.reshape(BLOCK_QUERIES, GROUP * HEAD_SIZE)
-    held = choose(4, scalars, moved, held, scalars)
+    held = choose(4, scalars, moved, held, scalars, cost(GROUP, CACHE_SLOTS))
     moved = from_earlier(held, 2)
     keys, vals = widen(kv_cache, q)
-    held = choose(2, scalars, moved, held, keys)
+    held = choose(2, scalars, moved, held, keys, slight)
     moved = from_earlier(held, 1)
     state = attend_local(scalars, q, keys, vals)
     result = attend_anchor(scalars, moved, held, q, *state)

time: 95.3 us -> 91.1 us (0.956)
  the two profiles are of different devices: /device:TPU:227 before, /device:TPU:163 now
where the time goes in v1:
time: 91.1 us; the launch traced here: 90.7 us
  Pallas kernels  44.3 us (49%)
  starting transfers between devices  19.5 us (21%)
  blocking collectives  17 us (19%)
  waiting for transfers between devices  5.67 us (6%)
  local copies, waits for them, and re-layouts  2.84 us (3%)
  between operations  1.41 us (2%)
    pallas_call x1, Pallas kernels, attend_local(): pl.pallas_call(local_kernel, out_shape=(jax.ShapeDtypeStruct((GROUP, BLOC...  37.1 us
    all_to_all x1, blocking collectives, body(): lax.all_to_all(result, 'head', split_axis=0, concat_axis=1, tiled=True)  17 us
    ppermute x3, starting transfers between devices, from_earlier(): lax.ppermute(held, 'ctx', [(b, b + shift) for b in range(blocks - shift)])  13.7 us
    all_to_all x1, starting transfers between devices, body(): lax.all_to_all(cut(queries, held), 'head', split_axis=0, concat_axis=0, t...  5.75 us
    pallas_call x1, Pallas kernels, attend_anchor(): pl.pallas_call(anchor_kernel, out_shape=jax.ShapeDtypeStruct(q.shape, jnp...  4.99 us
    all_to_all x1, waiting for transfers between devices, body(): lax.all_to_all(cut(queries, held), 'head', split_axis=0, concat_axis=0, t...  3.98 us
  transfers between devices with their start and end apart: 4, of which 2 were waited for; matrix products, arithmetic and copies ran while one was open for 0% of the time, Pallas kernels for 43%

profile of v1, /device:TPU:163, one launch (start us, length us, event | category | flops | bytes accessed | tf_op | source)
XLA Modules:
  0.0 90.7 jit_solution(15530287975998306378)
XLA Ops:
  0.0 1.0 %slice.3.after.held = bf16[2,512,128]{2,1,0:T(8,128)(2,1)S(1)} slice(bf16[2,2048,128]{2,1,0:T(8,128)(2,1)} %part_ref.1), slice={[0:2], [0:512], [0:128]} | slice | bytes 524288 | tf_op jit(solution)/shard_map/slice | solution.py:265
  1.0 3.5 %collective-permute-start = (bf16[2,512,128]{2,1,0:T(8,128)(2,1)S(1)}, bf16[2,512,128]{2,1,0:T(8,128)(2,1)S(1)}, u32[]{:S(2)}, u32[]{:S(2)}) collective-permute-start(bf16[2,512,128]{2,1,0:T(8,128)(2,1)S(1)} %slice.3.after.held), channel_id=1, source_target_pairs={{0,32},{8,40},{16,48},{24,56},{32,64},{40,72},{48,80},{56,88},{64,... | collective-permute-start | bytes 786440 | tf_op jit(solution)/shard_map/ppermute | solution.py:268
  4.5 0.0 copy-start
  4.5 1.0 %copy-done = bf16[32,8192]{1,0:T(8,128)(2,1)S(1)} copy-done((bf16[32,8192]{1,0:T(8,128)(2,1)S(1)}, bf16[32,8192]{1,0:T(8,128)(2,1)}, u32[]{:S(2)}) %copy-start) | copy-done | bytes 524312
  5.6 0.8 cut.1
  6.4 5.8 %all-to-all-start = ((bf16[8,32,1024]{2,1,0:T(8,128)(2,1)}), bf16[8,32,1024]{2,1,0:T(8,128)(2,1)S(1)}, u32[]{:S(2)}, u32[]{:S(2)}) async-start(bf16[8,32,1024]{2,1,0:T(8,128)(2,1)} %cut.1), calls=%async_computation | async-start | bytes 1048576 | tf_op jit(solution)/shard_map/all_to_all | solution.py:271
  13.5 0.1 pad_add_fusion.scalars.after
  13.5 0.0 copy-start.1
  13.5 0.0 collective-permute-done.moved
  13.6 0.6 choose.2.held
  14.1 4.4 %collective-permute-start.1 = (bf16[2,512,128]{2,1,0:T(8,128)(2,1)S(1)}, bf16[2,512,128]{2,1,0:T(8,128)(2,1)S(1)}, u32[]{:S(2)}, u32[]{:S(2)}) collective-permute-start(bf16[2,512,128]{2,1,0:T(8,128)(2,1)S(1)} %choose.2.held), channel_id=1, source_target_pairs={{0,16},{8,24},{16,32},{24,40},{32,48},{40,56},{48,64},{56,72},{64,... | collective-permute-start | bytes 786440 | tf_op jit(solution)/shard_map/ppermute | solution.py:268
  18.6 4.0 %all-to-all-done = bf16[8,32,1024]{2,1,0:T(8,128)(2,1)S(1)} async-done(((bf16[8,32,1024]{2,1,0:T(8,128)(2,1)}), bf16[8,32,1024]{2,1,0:T(8,128)(2,1)S(1)}, u32[]{:S(2)}, u32[]{:S(2)}) %all-to-all-start) | async-done | bytes 524320 | tf_op jit(solution)/shard_map/all_to_all | solution.py:271
  22.5 0.0 copy-done.1
  22.5 0.3 widen.1
  22.8 1.7 %collective-permute-done.1.moved = bf16[2,512,128]{2,1,0:T(8,128)(2,1)S(1)} collective-permute-done((bf16[2,512,128]{2,1,0:T(8,128)(2,1)S(1)}, bf16[2,512,128]{2,1,0:T(8,128)(2,1)S(1)}, u32[]{:S(2)}, u32[]{:S(2)}) %collective-permute-start.1) | collective-permute-done | bytes 262176 | tf_op jit(solution)/shard_map/ppermute | solution.py:268
  24.5 0.6 choose.3.held
  25.1 5.8 %collective-permute-start.2 = (bf16[2,512,128]{2,1,0:T(8,128)(2,1)S(1)}, bf16[2,512,128]{2,1,0:T(8,128)(2,1)S(1)}, u32[]{:S(2)}, u32[]{:S(2)}) collective-permute-start(bf16[2,512,128]{2,1,0:T(8,128)(2,1)S(1)} %choose.3.held), channel_id=1, source_target_pairs={{0,8},{8,16},{16,24},{24,32},{32,40},{40,48},{48,56},{56,64},{64,7... | collective-permute-start | bytes 786440 | tf_op jit(solution)/shard_map/ppermute | solution.py:268
  30.9 37.1 %attend_local.1 = (f32[8,256,256]{2,1,0:T(8,128)S(1)}, f32[8,256,128]{2,1,0:T(8,128)S(1)}, s32[1]{0:T(128)}) custom-call(s32[2]{0:T(128)S(1)} %pad_add_fusion.scalars.after, bf16[256,1024]{1,0:T(8,128)(2,1)S(1)} %bitcast.15, bf16[128,2048]{1,0:T(8,128)(2,1)S(1)} %get-tuple-element.10.keys.after, bf16[2048,256]{1,0:T(8,128)(2,1)S(1)} %get-tuple-element.11.vals), custom_call_target="tpu_custom_call" | custom-call | flops 2147483648 | bytes 2097152 | tf_op jit(solution)/shard_map/attend_local/pallas_call | solution.py:224
  67.9 0.0 collective-permute-done.2.moved
  67.9 5.0 %attend_anchor.1 = bf16[256,1024]{1,0:T(8,128)(2,1)S(1)} custom-call(s32[2]{0:T(128)S(1)} %pad_add_fusion.scalars.after, s32[1]{0:T(128)} %get-tuple-element.12.safe, bf16[2,512,128]{2,1,0:T(8,128)(2,1)S(1)} %collective-permute-done.2.moved, bf16[2,512,128]{2,1,0:T(8,128)(2,1)S(1)} %choose.3.held, bf16[256,1024]{1,0:T(8,128)(2,1)S(1)} %bitcast.16, ...), custom_call_target="tpu_custom_call" | custom-call | flops 536870912 | bytes 2097152 | tf_op jit(solution)/shard_map/attend_anchor/pallas_call | solution.py:244
  72.9 17.0 %all_to_all.24 = bf16[8,32,1024]{2,1,0:T(8,128)(2,1)S(1)} all-to-all(bf16[8,32,1024]{2,1,0:T(8,128)(2,1)S(1)} %bitcast.17), channel_id=1, replica_groups=mesh['ctx'=64,'head'=8] {'head'}, dimensions={0} | all-to-all | bytes 1048576 | tf_op jit(solution)/shard_map/all_to_all | solution.py:280
  89.9 0.8 copy.6
Async XLA Ops:
  1.0 12.6 %collective-permute-start = (bf16[2,512,128]{2,1,0:T(8,128)(2,1)S(1)}, bf16[2,512,128]{2,1,0:T(8,128)(2,1)S(1)}, u32[]{:S(2)}, u32[]{:S(2)}) collective-permute-start(bf16[2,512,128]{2,1,0:T(8,128)(2,1)S(1)} %slice.3.after.held), channel_id=1, source_target_pairs={{0,32},{8,40},{16,48},{24,56},{32,64},{40,72},{48,80},{56,88},{64,... | collective-permute-start | bytes 786440 | tf_op jit(solution)/shard_map/ppermute | solution.py:268
  4.5 1.0 %copy-start = (bf16[32,8192]{1,0:T(8,128)(2,1)S(1)}, bf16[32,8192]{1,0:T(8,128)(2,1)}, u32[]{:S(2)}) copy-start(bf16[32,8192]{1,0:T(8,128)(2,1)} %queries.1) | copy-start | bytes 1572868
  6.4 16.1 %all-to-all-start = ((bf16[8,32,1024]{2,1,0:T(8,128)(2,1)}), bf16[8,32,1024]{2,1,0:T(8,128)(2,1)S(1)}, u32[]{:S(2)}, u32[]{:S(2)}) async-start(bf16[8,32,1024]{2,1,0:T(8,128)(2,1)} %cut.1), calls=%async_computation | async-start | bytes 1048576 | tf_op jit(solution)/shard_map/all_to_all | solution.py:271
  13.5 9.0 %copy-start.1 = (bf16[2,2048,128]{2,1,0:T(8,128)(2,1)S(1)}, bf16[2,2048,128]{2,1,0:T(8,128)(2,1)}, u32[]{:S(2)}) copy-start(bf16[2,2048,128]{2,1,0:T(8,128)(2,1)} %part_ref.1) | copy-start | bytes 3145732
  14.1 10.4 %collective-permute-start.1 = (bf16[2,512,128]{2,1,0:T(8,128)(2,1)S(1)}, bf16[2,512,128]{2,1,0:T(8,128)(2,1)S(1)}, u32[]{:S(2)}, u32[]{:S(2)}) collective-permute-start(bf16[2,512,128]{2,1,0:T(8,128)(2,1)S(1)} %choose.2.held), channel_id=1, source_target_pairs={{0,16},{8,24},{16,32},{24,40},{32,48},{40,56},{48,64},{56,72},{64,... | collective-permute-start | bytes 786440 | tf_op jit(solution)/shard_map/ppermute | solution.py:268
  25.1 42.8 %collective-permute-start.2 = (bf16[2,512,128]{2,1,0:T(8,128)(2,1)S(1)}, bf16[2,512,128]{2,1,0:T(8,128)(2,1)S(1)}, u32[]{:S(2)}, u32[]{:S(2)}) collective-permute-start(bf16[2,512,128]{2,1,0:T(8,128)(2,1)S(1)} %choose.3.held), channel_id=1, source_target_pairs={{0,8},{8,16},{16,24},{24,32},{32,40},{40,48},{48,56},{56,64},{64,7... | collective-permute-start | bytes 786440 | tf_op jit(solution)/shard_map/ppermute | solution.py:268

commit v2 on v0

v2 whole, which is shorter than its diff:
```python
import functools
import math

import jax
import jax.numpy as jnp
from jax import lax
from jax.experimental import pallas as pl
from jax.experimental.pallas import tpu as pltpu
from jax.sharding import PartitionSpec as P

QUERY_HEAD_COUNT = 64
KEY_HEADS = 8
HEAD_SIZE = 128
GROUP = QUERY_HEAD_COUNT // KEY_HEADS
BLOCK_QUERIES = 256
CACHE_SLOTS = 2048
ANCHOR_SLOTS = 512
SPAN = 8
TILE = 256
STACK = 2
CHUNK = 512

masked_score = -1e30
EXP2_SCALE = math.log2(math.e) / math.sqrt(HEAD_SIZE)
SAFE_LOW, SAFE_HIGH = 2.0**-60, 2.0**60


def head_columns(g):
    return slice(g * HEAD_SIZE, (g + 1) * HEAD_SIZE)


def cut_kernel(queries, after, outgoing):
    pieces, _, width = outgoing.shape
    for h in range(pieces):
        outgoing[h] = queries[:, h * width:(h + 1) * width]


def choose_kernel(shift, scalars, moved, held, after, out):
    arrived = (scalars[1] & shift) != 0

    @pl.when(arrived)
    def _():
        out[...] = moved[...]

    @pl.when(jnp.logical_not(arrived))
    def _():
        out[...] = held[...]


def widen_kernel(part_ref, after, keys, vals):
    widen_into(part_ref, keys, vals)


def widen_into(part_ref, keys, vals):
    keys[...] = part_ref[0].astype(jnp.float32).T.astype(jnp.bfloat16)
    vals[:, 0:HEAD_SIZE] = part_ref[1]
    vals[:, HEAD_SIZE:] = jnp.ones(part_ref.shape[1:], jnp.bfloat16)


def scaled_scores(q, keys):
    return jnp.dot(q, keys, preferred_element_type=jnp.float32) * EXP2_SCALE


def stacked(q_ref, stack):
    return jnp.concatenate([q_ref[:, head_columns(stack * STACK + g)] for g in range(STACK)], axis=0)


def rows_of(g):
    return slice(g * BLOCK_QUERIES, (g + 1) * BLOCK_QUERIES)


def tile_of(tile):
    return slice(tile * TILE, (tile + 1) * TILE)


def tile_at(tile):
    return pl.ds(pl.multiple_of(tile * TILE, TILE), TILE)


def causal_slant():
    row = lax.broadcasted_iota(jnp.int32, (BLOCK_QUERIES, TILE), 0)
    col = lax.broadcasted_iota(jnp.int32, (BLOCK_QUERIES, TILE), 1)
    return col - row


def local_kernel(scalars, q_ref, keys, vals, state_ref, weights):
    stacks = state_ref.shape[0] // STACK
    full_tiles = scalars[0]
    slant = causal_slant()

    def attend(chunks):
        span = chunks * CHUNK
        tiles = span // TILE

        def weigh(stack):
            q = stacked(q_ref, stack)
            for tile in range(tiles):
                s = scaled_scores(q, keys[:, tile_of(tile)])
                if tile * TILE >= span - CHUNK:
                    allowed = slant <= (full_tiles - tile) * TILE
                    s = jnp.where(jnp.concatenate([allowed] * STACK, axis=0), s, masked_score)
                weights[stack % 2, :, tile_of(tile)] = jnp.exp2(s).astype(jnp.bfloat16)

        weigh(0)
        for stack in range(stacks):
            if stack + 1 < stacks:
                weigh(stack + 1)
            mixed = jnp.dot(weights[stack % 2, :, 0:span], vals[0:span, :], preferred_element_type=jnp.float32)
            for g in range(STACK):
                state_ref[stack * STACK + g] = mixed[rows_of(g)]

    for chunks in range(1, CACHE_SLOTS // CHUNK + 1):
        pl.when(full_tiles * TILE // CHUNK == chunks - 1)(functools.partial(attend, chunks))


def exact_head(g, full_tiles, has_anchor, q_ref, local, anchor, scores):
    q = q_ref[:, head_columns(g)]
    slant = causal_slant()
    base = ANCHOR_SLOTS // TILE
    zero = jnp.zeros((BLOCK_QUERIES, 2 * HEAD_SIZE), jnp.float32)

    def score_into(slot, keys, tile, allowed, peak):
        s = jnp.where(allowed, scaled_scores(q, keys[:, tile_at(tile)]), masked_score)
        scores[:, tile_at(slot + tile)] = s
        return jnp.maximum(peak, jnp.max(s, axis=1, keepdims=True))

    def mix_from(slot, vals, tile, mixed):
        p = jnp.exp2(scores[:, tile_at(slot + tile)] - peak).astype(jnp.bfloat16)
        return mixed + jnp.dot(p, vals[tile_at(tile), :], preferred_element_type=jnp.float32)

    peak = jnp.full((BLOCK_QUERIES, 1), masked_score, jnp.float32)
    peak = lax.fori_loop(
        0, full_tiles + 1,
        lambda tile, peak: score_into(base, local[0], tile, slant <= (full_tiles - tile) * TILE, peak), peak)
    peak = lax.fori_loop(
        0, base, lambda tile, peak: score_into(0, anchor[0], tile, jnp.logical_and(has_anchor, slant == slant), peak),
        peak)
    mixed = lax.fori_loop(0, full_tiles + 1, functools.partial(mix_from, base, local[1]), zero)
    return lax.fori_loop(0, base, functools.partial(mix_from, 0, anchor[1]), mixed)


def anchor_kernel(scalars, moved, held, q_ref, local_keys, local_vals, states, out_ref,
                  anchor, keys, vals, weights, scores):
    heads = states.shape[0]
    has_anchor = scalars[1] > 0
    choose_kernel(1, scalars, moved, held, None, anchor)
    widen_into(anchor, keys, vals)

    def write(g, mixed):
        out_ref[:, head_columns(g)] = (mixed[:, :HEAD_SIZE] / mixed[:, HEAD_SIZE:]).astype(jnp.bfloat16)

    for stack in range(heads // STACK):
        s = jnp.where(has_anchor, scaled_scores(stacked(q_ref, stack), keys[...]), masked_score)
        weights[stack] = jnp.exp2(s).astype(jnp.bfloat16)
    low = high = None
    for stack in range(heads // STACK):
        both = jnp.dot(weights[stack], vals[...], preferred_element_type=jnp.float32)
        for g in range(STACK):
            state = states[stack * STACK + g]
            mixed = both[rows_of(g)] + state
            write(stack * STACK + g, mixed)
            below, above = state[:, HEAD_SIZE:], mixed[:, HEAD_SIZE:]
            low = below if low is None else jnp.minimum(low, below)
            high = above if high is None else jnp.maximum(high, above)
    safe = jnp.logical_and(jnp.min(low) > SAFE_LOW, jnp.max(high) < SAFE_HIGH)

    @pl.when(jnp.logical_not(safe))
    def _():
        for g in range(heads):
            write(g, exact_head(g, scalars[0], has_anchor, q_ref, (local_keys, local_vals), (keys, vals), scores))


def cost(heads, keys):
    flops = 4 * BLOCK_QUERIES * heads * keys * HEAD_SIZE
    return pl.CostEstimate(flops=flops, bytes_accessed=2 * 2**20, transcendentals=flops // 512)


smem = pl.BlockSpec(memory_space=pltpu.SMEM)
vmem = pl.BlockSpec(memory_space=pltpu.VMEM)
anywhere = pl.BlockSpec(memory_space=pl.ANY)
small = pltpu.CompilerParams(vmem_limit_bytes=4 * 2**20)
params = pltpu.CompilerParams(vmem_limit_bytes=24 * 2**20)
slight = pl.CostEstimate(flops=1000, bytes_accessed=1000, transcendentals=0)


def wide_shapes(count):
    return (jax.ShapeDtypeStruct((HEAD_SIZE, count), jnp.bfloat16),
            jax.ShapeDtypeStruct((count, 2 * HEAD_SIZE), jnp.bfloat16))


def cut(queries, after):
    rows, width = queries.shape
    return pl.pallas_call(
        cut_kernel,
        out_shape=jax.ShapeDtypeStruct((KEY_HEADS, rows, width // KEY_HEADS), jnp.bfloat16),
        in_specs=[vmem, anywhere],
        out_specs=vmem,
        compiler_params=small,
        cost_estimate=slight,
        name="cut",
    )(queries, after)


def choose(shift, scalars, moved, held, after, estimate):
    return pl.pallas_call(
        functools.partial(choose_kernel, shift),
        out_shape=jax.ShapeDtypeStruct(held.shape, held.dtype),
        in_specs=[smem, vmem, vmem, anywhere],
        out_specs=vmem,
        compiler_params=small,
        cost_estimate=estimate,
        name="choose",
    )(scalars, moved, held, after)


def widen(kv, after):
    return pl.pallas_call(
        widen_kernel,
        out_shape=wide_shapes(CACHE_SLOTS),
        in_specs=[vmem, anywhere],
        out_specs=(vmem, vmem),
        compiler_params=params,
        cost_estimate=cost(GROUP, CACHE_SLOTS),
        name="widen",
    )(kv, after)


def attend_local(scalars, q, keys, vals):
    return pl.pallas_call(
        local_kernel,
        out_shape=jax.ShapeDtypeStruct((GROUP, BLOCK_QUERIES, 2 * HEAD_SIZE), jnp.float32),
        in_specs=[smem, vmem, vmem, vmem],
        out_specs=vmem,
        scratch_shapes=[pltpu.VMEM((2, STACK * BLOCK_QUERIES, CACHE_SLOTS), jnp.bfloat16)],
        compiler_params=params,
        cost_estimate=cost(GROUP, CACHE_SLOTS),
        name="attend_local",
    )(scalars, q, keys, vals)


def attend_anchor(scalars, moved, held, q, keys, vals, states):
    return pl.pallas_call(
        anchor_kernel,
        out_shape=jax.ShapeDtypeStruct(q.shape, jnp.bfloat16),
        in_specs=[smem] + [vmem] * 6,
        out_specs=vmem,
        scratch_shapes=[
            pltpu.VMEM(held.shape, held.dtype),
            *(pltpu.VMEM(wide.shape, wide.dtype) for wide in wide_shapes(ANCHOR_SLOTS)),
            pltpu.VMEM((GROUP // STACK, STACK * BLOCK_QUERIES, ANCHOR_SLOTS), jnp.bfloat16),
            pltpu.VMEM((BLOCK_QUERIES, ANCHOR_SLOTS + CACHE_SLOTS), jnp.float32),
        ],
        compiler_params=params,
        cost_estimate=cost(GROUP, ANCHOR_SLOTS),
        name="attend_anchor",
    )(scalars, moved, held, q, keys, vals, states)


def body(queries, kv_cache, anchor_src, stretch_pos):
    block = lax.axis_index("ctx").astype(jnp.int32)
    blocks = lax.axis_size("ctx")
    scalars = jnp.stack([stretch_pos[0] // TILE, block - anchor_src[0]])
    held = lax.optimization_barrier(kv_cache[:, :ANCHOR_SLOTS, :])

    def from_earlier(held, shift):
        return lax.ppermute(held, "ctx", [(b, b + shift) for b in range(blocks - shift)])

    moved = from_earlier(held, 4)
    q = lax.all_to_all(cut(queries, held), "head", split_axis=0, concat_axis=0, tiled=True)
    q = q.reshape(BLOCK_QUERIES, GROUP * HEAD_SIZE)
    held = choose(4, scalars, moved, held, scalars, cost(GROUP, CACHE_SLOTS))
    moved = from_earlier(held, 2)
    keys, vals = widen(kv_cache, q)
    held = choose(2, scalars, moved, held, keys, slight)
    moved = from_earlier(held, 1)
    states = attend_local(scalars, q, keys, vals)
    result = attend_anchor(scalars, moved, held, q, keys, vals, states)
    return lax.all_to_all(result, "head", split_axis=0, concat_axis=1, tiled=True)


def solution(mesh):
    in_specs = (P(("ctx", "head"), None), P(None, "ctx", "head"), P("ctx"), P("ctx"))
    out_specs = P(("ctx", "head"), None)
    return jax.shard_map(body, mesh=mesh, in_specs=in_specs, out_specs=out_specs, check_vma=False)
```

time: 95.3 us -> 95.8 us (level)
  the two profiles are of different devices: /device:TPU:227 before, /device:TPU:128 now
where the time goes in v2:
time: 95.8 us; the launch traced here: 95.5 us
  Pallas kernels  47.9 us (50%)
  blocking collectives  16.9 us (18%)
  starting transfers between devices  15.2 us (16%)
  waiting for transfers between devices  11.1 us (12%)
  local copies, waits for them, and re-layouts  2.84 us (3%)
  between operations  1.4 us (1%)
    pallas_call x1, Pallas kernels, attend_anchor(): pl.pallas_call(anchor_kernel, out_shape=jax.ShapeDtypeStruct(q.shape, jnp...  40.3 us
    all_to_all x1, blocking collectives, body(): lax.all_to_all(result, 'head', split_axis=0, concat_axis=1, tiled=True)  16.9 us
    ppermute x3, starting transfers between devices, from_earlier(): lax.ppermute(held, 'ctx', [(b, b + shift) for b in range(blocks - shift)])  8.25 us
    all_to_all x1, waiting for transfers between devices, body(): lax.all_to_all(cut(queries, held), 'head', split_axis=0, concat_axis=0, t...  7.79 us
    all_to_all x1, starting transfers between devices, body(): lax.all_to_all(cut(queries, held), 'head', split_axis=0, concat_axis=0, t...  6.93 us
    pallas_call x1, Pallas kernels, attend_local(): pl.pallas_call(local_kernel, out_shape=jax.ShapeDtypeStruct((GROUP, BLOCK...  5.42 us
    ppermute x3, waiting for transfers between devices, from_earlier(): lax.ppermute(held, 'ctx', [(b, b + shift) for b in range(blocks - shift)])  3.34 us
  transfers between devices with their start and end apart: 4, of which 3 were waited for; matrix products, arithmetic and copies ran while one was open for 0% of the time, Pallas kernels for 7%

profile of v2, /device:TPU:128, one launch (start us, length us, event | category | flops | bytes accessed | tf_op | source)
XLA Modules:
  0.0 95.5 jit_solution(7686086461101387203)
XLA Ops:
  0.0 1.0 %slice.3.held.after = bf16[2,512,128]{2,1,0:T(8,128)(2,1)S(1)} slice(bf16[2,2048,128]{2,1,0:T(8,128)(2,1)} %part_ref.1), slice={[0:2], [0:512], [0:128]} | slice | bytes 524288 | tf_op jit(solution)/shard_map/slice | solution.py:263
  1.0 3.8 %collective-permute-start = (bf16[2,512,128]{2,1,0:T(8,128)(2,1)S(1)}, bf16[2,512,128]{2,1,0:T(8,128)(2,1)S(1)}, u32[]{:S(2)}, u32[]{:S(2)}) collective-permute-start(bf16[2,512,128]{2,1,0:T(8,128)(2,1)S(1)} %slice.3.held.after), channel_id=1, source_target_pairs={{0,32},{8,40},{16,48},{24,56},{32,64},{40,72},{48,80},{56,88},{64,... | collective-permute-start | bytes 786440 | tf_op jit(solution)/shard_map/ppermute | solution.py:266
  4.8 0.0 copy-start
  4.8 1.0 %copy-done = bf16[32,8192]{1,0:T(8,128)(2,1)S(1)} copy-done((bf16[32,8192]{1,0:T(8,128)(2,1)S(1)}, bf16[32,8192]{1,0:T(8,128)(2,1)}, u32[]{:S(2)}) %copy-start) | copy-done | bytes 524312
  5.9 0.8 cut.1
  6.7 6.9 %all-to-all-start = ((bf16[8,32,1024]{2,1,0:T(8,128)(2,1)}), bf16[8,32,1024]{2,1,0:T(8,128)(2,1)S(1)}, u32[]{:S(2)}, u32[]{:S(2)}) async-start(bf16[8,32,1024]{2,1,0:T(8,128)(2,1)} %cut.1), calls=%async_computation | async-start | bytes 1048576 | tf_op jit(solution)/shard_map/all_to_all | solution.py:269
  14.9 0.1 pad_add_fusion.scalars.after
  15.0 0.0 copy-start.1
  15.0 0.0 collective-permute-done.moved
  15.0 0.6 choose.2.held
  15.6 2.5 %collective-permute-start.1 = (bf16[2,512,128]{2,1,0:T(8,128)(2,1)S(1)}, bf16[2,512,128]{2,1,0:T(8,128)(2,1)S(1)}, u32[]{:S(2)}, u32[]{:S(2)}) collective-permute-start(bf16[2,512,128]{2,1,0:T(8,128)(2,1)S(1)} %choose.2.held), channel_id=1, source_target_pairs={{0,16},{8,24},{16,32},{24,40},{32,48},{40,56},{48,64},{56,72},{64,... | collective-permute-start | bytes 786440 | tf_op jit(solution)/shard_map/ppermute | solution.py:266
  18.1 7.8 %all-to-all-done = bf16[8,32,1024]{2,1,0:T(8,128)(2,1)S(1)} async-done(((bf16[8,32,1024]{2,1,0:T(8,128)(2,1)}), bf16[8,32,1024]{2,1,0:T(8,128)(2,1)S(1)}, u32[]{:S(2)}, u32[]{:S(2)}) %all-to-all-start) | async-done | bytes 524320 | tf_op jit(solution)/shard_map/all_to_all | solution.py:269
  25.9 0.0 copy-done.1
  25.9 0.3 widen.1
  26.2 0.9 collective-permute-done.1.moved
  27.1 0.6 choose.3.held
  27.6 1.9 %collective-permute-start.2 = (bf16[2,512,128]{2,1,0:T(8,128)(2,1)S(1)}, bf16[2,512,128]{2,1,0:T(8,128)(2,1)S(1)}, u32[]{:S(2)}, u32[]{:S(2)}) collective-permute-start(bf16[2,512,128]{2,1,0:T(8,128)(2,1)S(1)} %choose.3.held), channel_id=1, source_target_pairs={{0,8},{8,16},{16,24},{24,32},{32,40},{40,48},{48,56},{56,64},{64,7... | collective-permute-start | bytes 786440 | tf_op jit(solution)/shard_map/ppermute | solution.py:266
  29.6 5.4 %attend_local.1.states = f32[8,256,256]{2,1,0:T(8,128)S(1)} custom-call(s32[2]{0:T(128)S(1)} %pad_add_fusion.scalars.after, bf16[256,1024]{1,0:T(8,128)(2,1)S(1)} %bitcast.15, bf16[128,2048]{1,0:T(8,128)(2,1)S(1)} %get-tuple-element.7.after.keys.local_keys, bf16[2048,256]{1,0:T(8,128)(2,1)S(1)} %get-tuple-element.8.vals.local_vals), custom_call_target="tpu_custom_call" | custom-call | flops 2147483648 | bytes 2097152 | tf_op jit(solution)/shard_map/attend_local/pallas_call | solution.py:229
  35.0 2.4 %collective-permute-done.2.moved = bf16[2,512,128]{2,1,0:T(8,128)(2,1)S(1)} collective-permute-done((bf16[2,512,128]{2,1,0:T(8,128)(2,1)S(1)}, bf16[2,512,128]{2,1,0:T(8,128)(2,1)S(1)}, u32[]{:S(2)}, u32[]{:S(2)}) %collective-permute-start.2) | collective-permute-done | bytes 262176 | tf_op jit(solution)/shard_map/ppermute | solution.py:266
  37.4 40.3 %attend_anchor.1 = bf16[256,1024]{1,0:T(8,128)(2,1)S(1)} custom-call(s32[2]{0:T(128)S(1)} %pad_add_fusion.scalars.after, bf16[2,512,128]{2,1,0:T(8,128)(2,1)S(1)} %collective-permute-done.2.moved, bf16[2,512,128]{2,1,0:T(8,128)(2,1)S(1)} %choose.3.held, bf16[256,1024]{1,0:T(8,128)(2,1)S(1)} %bitcast.16, ...), custom_call_target="tpu_custom_call" | custom-call | flops 536870912 | bytes 2097152 | tf_op jit(solution)/shard_map/attend_anchor/pallas_call | solution.py:242
  77.7 16.9 %all_to_all.24 = bf16[8,32,1024]{2,1,0:T(8,128)(2,1)S(1)} all-to-all(bf16[8,32,1024]{2,1,0:T(8,128)(2,1)S(1)} %bitcast.17), channel_id=1, replica_groups=mesh['ctx'=64,'head'=8] {'head'}, dimensions={0} | all-to-all | bytes 1048576 | tf_op jit(solution)/shard_map/all_to_all | solution.py:278
  94.6 0.8 copy.6
Async XLA Ops:
  1.0 14.0 %collective-permute-start = (bf16[2,512,128]{2,1,0:T(8,128)(2,1)S(1)}, bf16[2,512,128]{2,1,0:T(8,128)(2,1)S(1)}, u32[]{:S(2)}, u32[]{:S(2)}) collective-permute-start(bf16[2,512,128]{2,1,0:T(8,128)(2,1)S(1)} %slice.3.held.after), channel_id=1, source_target_pairs={{0,32},{8,40},{16,48},{24,56},{32,64},{40,72},{48,80},{56,88},{64,... | collective-permute-start | bytes 786440 | tf_op jit(solution)/shard_map/ppermute | solution.py:266
  4.8 1.0 %copy-start = (bf16[32,8192]{1,0:T(8,128)(2,1)S(1)}, bf16[32,8192]{1,0:T(8,128)(2,1)}, u32[]{:S(2)}) copy-start(bf16[32,8192]{1,0:T(8,128)(2,1)} %queries.1) | copy-start | bytes 1572868
  6.7 19.2 %all-to-all-start = ((bf16[8,32,1024]{2,1,0:T(8,128)(2,1)}), bf16[8,32,1024]{2,1,0:T(8,128)(2,1)S(1)}, u32[]{:S(2)}, u32[]{:S(2)}) async-start(bf16[8,32,1024]{2,1,0:T(8,128)(2,1)} %cut.1), calls=%async_computation | async-start | bytes 1048576 | tf_op jit(solution)/shard_map/all_to_all | solution.py:269
  15.0 10.9 %copy-start.1 = (bf16[2,2048,128]{2,1,0:T(8,128)(2,1)S(1)}, bf16[2,2048,128]{2,1,0:T(8,128)(2,1)}, u32[]{:S(2)}) copy-start(bf16[2,2048,128]{2,1,0:T(8,128)(2,1)} %part_ref.1) | copy-start | bytes 3145732
  15.6 11.5 %collective-permute-start.1 = (bf16[2,512,128]{2,1,0:T(8,128)(2,1)S(1)}, bf16[2,512,128]{2,1,0:T(8,128)(2,1)S(1)}, u32[]{:S(2)}, u32[]{:S(2)}) collective-permute-start(bf16[2,512,128]{2,1,0:T(8,128)(2,1)S(1)} %choose.2.held), channel_id=1, source_target_pairs={{0,16},{8,24},{16,32},{24,40},{32,48},{40,56},{48,64},{56,72},{64,... | collective-permute-start | bytes 786440 | tf_op jit(solution)/shard_map/ppermute | solution.py:266
  27.6 9.8 %collective-permute-start.2 = (bf16[2,512,128]{2,1,0:T(8,128)(2,1)S(1)}, bf16[2,512,128]{2,1,0:T(8,128)(2,1)S(1)}, u32[]{:S(2)}, u32[]{:S(2)}) collective-permute-start(bf16[2,512,128]{2,1,0:T(8,128)(2,1)S(1)} %choose.3.held), channel_id=1, source_target_pairs={{0,8},{8,16},{16,24},{24,32},{32,40},{40,48},{48,56},{56,64},{64,7... | collective-permute-start | bytes 786440 | tf_op jit(solution)/shard_map/ppermute | solution.py:266

commit v3 on v2

--- a/solution.py
+++ b/solution.py
@@ -265,13 +265,13 @@
     def from_earlier(held, shift):
         return lax.ppermute(held, "ctx", [(b, b + shift) for b in range(blocks - shift)])
 
-    moved = from_earlier(held, 4)
+    moved = from_earlier(held, 2)
     q = lax.all_to_all(cut(queries, held), "head", split_axis=0, concat_axis=0, tiled=True)
     q = q.reshape(BLOCK_QUERIES, GROUP * HEAD_SIZE)
-    held = choose(4, scalars, moved, held, scalars, cost(GROUP, CACHE_SLOTS))
-    moved = from_earlier(held, 2)
-    keys, vals = widen(kv_cache, q)
-    held = choose(2, scalars, moved, held, keys, slight)
+    held = choose(2, scalars, moved, held, scalars, cost(GROUP, CACHE_SLOTS))
+    moved = from_earlier(held, 4)
+    keys, vals = widen(kv_cache, held)
+    held = choose(4, scalars, moved, held, keys, slight)
     moved = from_earlier(held, 1)
     states = attend_local(scalars, q, keys, vals)
     result = attend_anchor(scalars, moved, held, q, keys, vals, states)

time: 95.8 us -> 94.4 us (0.985)
  the two profiles are of different devices: /device:TPU:128 before, /device:TPU:33 now
where the time goes in v3:
time: 94.4 us; the launch traced here: 94 us
  Pallas kernels  47.8 us (51%)
  blocking collectives  19 us (20%)
  starting transfers between devices  18.3 us (19%)
  waiting for transfers between devices  4.6 us (5%)
  local copies, waits for them, and re-layouts  2.84 us (3%)
  between operations  1.42 us (2%)
    pallas_call x1, Pallas kernels, attend_anchor(): pl.pallas_call(anchor_kernel, out_shape=jax.ShapeDtypeStruct(q.shape, jnp...  40.2 us
    all_to_all x1, blocking collectives, body(): lax.all_to_all(result, 'head', split_axis=0, concat_axis=1, tiled=True)  19 us
    ppermute x3, starting transfers between devices, from_earlier(): lax.ppermute(held, 'ctx', [(b, b + shift) for b in range(blocks - shift)])  11.9 us
    all_to_all x1, starting transfers between devices, body(): lax.all_to_all(cut(queries, held), 'head', split_axis=0, concat_axis=0, t...  6.36 us
    pallas_call x1, Pallas kernels, attend_local(): pl.pallas_call(local_kernel, out_shape=jax.ShapeDtypeStruct((GROUP, BLOCK...  5.38 us
    ppermute x3, waiting for transfers between devices, from_earlier(): lax.ppermute(held, 'ctx', [(b, b + shift) for b in range(blocks - shift)])  4.6 us
  transfers between devices with their start and end apart: 4, of which 1 were waited for; matrix products, arithmetic and copies ran while one was open for 0% of the time, Pallas kernels for 8%

profile of v3, /device:TPU:33, one launch (start us, length us, event | category | flops | bytes accessed | tf_op | source)
XLA Modules:
  0.0 94.0 jit_solution(18304038298608781862)
XLA Ops:
  0.0 1.0 %slice.3.held.after = bf16[2,512,128]{2,1,0:T(8,128)(2,1)S(1)} slice(bf16[2,2048,128]{2,1,0:T(8,128)(2,1)} %part_ref.1), slice={[0:2], [0:512], [0:128]} | slice | bytes 524288 | tf_op jit(solution)/shard_map/slice | solution.py:263
  1.0 3.1 %collective-permute-start = (bf16[2,512,128]{2,1,0:T(8,128)(2,1)S(1)}, bf16[2,512,128]{2,1,0:T(8,128)(2,1)S(1)}, u32[]{:S(2)}, u32[]{:S(2)}) collective-permute-start(bf16[2,512,128]{2,1,0:T(8,128)(2,1)S(1)} %slice.3.held.after), channel_id=1, source_target_pairs={{0,16},{8,24},{16,32},{24,40},{32,48},{40,56},{48,64},{56,72},{64,... | collective-permute-start | bytes 786440 | tf_op jit(solution)/shard_map/ppermute | solution.py:266
  4.1 0.0 copy-start
  4.1 1.0 %copy-done = bf16[32,8192]{1,0:T(8,128)(2,1)S(1)} copy-done((bf16[32,8192]{1,0:T(8,128)(2,1)S(1)}, bf16[32,8192]{1,0:T(8,128)(2,1)}, u32[]{:S(2)}) %copy-start) | copy-done | bytes 524312
  5.1 0.8 cut.1
  6.0 6.4 %all-to-all-start = ((bf16[8,32,1024]{2,1,0:T(8,128)(2,1)}), bf16[8,32,1024]{2,1,0:T(8,128)(2,1)S(1)}, u32[]{:S(2)}, u32[]{:S(2)}) async-start(bf16[8,32,1024]{2,1,0:T(8,128)(2,1)} %cut.1), calls=%async_computation | async-start | bytes 1048576 | tf_op jit(solution)/shard_map/all_to_all | solution.py:269
  13.6 0.1 pad_add_fusion.scalars.after
  13.7 0.0 copy-start.1
  13.7 0.0 collective-permute-done.moved
  13.7 0.6 choose.2.after.held
  14.3 3.5 %collective-permute-start.1 = (bf16[2,512,128]{2,1,0:T(8,128)(2,1)S(1)}, bf16[2,512,128]{2,1,0:T(8,128)(2,1)S(1)}, u32[]{:S(2)}, u32[]{:S(2)}) collective-permute-start(bf16[2,512,128]{2,1,0:T(8,128)(2,1)S(1)} %choose.2.after.held), channel_id=1, source_target_pairs={{0,32},{8,40},{16,48},{24,56},{32,64},{40,72},{48,80},{56,88},{64,... | collective-permute-start | bytes 786440 | tf_op jit(solution)/shard_map/ppermute | solution.py:266
  17.9 0.0 copy-done.1
  17.9 0.3 widen.1
  18.2 4.6 %collective-permute-done.1.moved = bf16[2,512,128]{2,1,0:T(8,128)(2,1)S(1)} collective-permute-done((bf16[2,512,128]{2,1,0:T(8,128)(2,1)S(1)}, bf16[2,512,128]{2,1,0:T(8,128)(2,1)S(1)}, u32[]{:S(2)}, u32[]{:S(2)}) %collective-permute-start.1) | collective-permute-done | bytes 262176 | tf_op jit(solution)/shard_map/ppermute | solution.py:266
  22.8 0.6 choose.3.held
  23.3 5.3 %collective-permute-start.2 = (bf16[2,512,128]{2,1,0:T(8,128)(2,1)S(1)}, bf16[2,512,128]{2,1,0:T(8,128)(2,1)S(1)}, u32[]{:S(2)}, u32[]{:S(2)}) collective-permute-start(bf16[2,512,128]{2,1,0:T(8,128)(2,1)S(1)} %choose.3.held), channel_id=1, source_target_pairs={{0,8},{8,16},{16,24},{24,32},{32,40},{40,48},{48,56},{56,64},{64,7... | collective-permute-start | bytes 786440 | tf_op jit(solution)/shard_map/ppermute | solution.py:266
  28.6 0.0 all-to-all-done
  28.6 5.4 %attend_local.1.states = f32[8,256,256]{2,1,0:T(8,128)S(1)} custom-call(s32[2]{0:T(128)S(1)} %pad_add_fusion.scalars.after, bf16[256,1024]{1,0:T(8,128)(2,1)S(1)} %bitcast.14, bf16[128,2048]{1,0:T(8,128)(2,1)S(1)} %get-tuple-element.7.after.keys.local_keys, bf16[2048,256]{1,0:T(8,128)(2,1)S(1)} %get-tuple-element.8.vals.local_vals), custom_call_target="tpu_custom_call" | custom-call | flops 2147483648 | bytes 2097152 | tf_op jit(solution)/shard_map/attend_local/pallas_call | solution.py:229
  34.0 0.0 collective-permute-done.2.moved
  34.0 40.2 %attend_anchor.1 = bf16[256,1024]{1,0:T(8,128)(2,1)S(1)} custom-call(s32[2]{0:T(128)S(1)} %pad_add_fusion.scalars.after, bf16[2,512,128]{2,1,0:T(8,128)(2,1)S(1)} %collective-permute-done.2.moved, bf16[2,512,128]{2,1,0:T(8,128)(2,1)S(1)} %choose.3.held, bf16[256,1024]{1,0:T(8,128)(2,1)S(1)} %bitcast.15, ...), custom_call_target="tpu_custom_call" | custom-call | flops 536870912 | bytes 2097152 | tf_op jit(solution)/shard_map/attend_anchor/pallas_call | solution.py:242
  74.2 19.0 %all_to_all.24 = bf16[8,32,1024]{2,1,0:T(8,128)(2,1)S(1)} all-to-all(bf16[8,32,1024]{2,1,0:T(8,128)(2,1)S(1)} %bitcast.16), channel_id=1, replica_groups=mesh['ctx'=64,'head'=8] {'head'}, dimensions={0} | all-to-all | bytes 1048576 | tf_op jit(solution)/shard_map/all_to_all | solution.py:278
  93.2 0.8 copy.6
Async XLA Ops:
  1.0 12.8 %collective-permute-start = (bf16[2,512,128]{2,1,0:T(8,128)(2,1)S(1)}, bf16[2,512,128]{2,1,0:T(8,128)(2,1)S(1)}, u32[]{:S(2)}, u32[]{:S(2)}) collective-permute-start(bf16[2,512,128]{2,1,0:T(8,128)(2,1)S(1)} %slice.3.held.after), channel_id=1, source_target_pairs={{0,16},{8,24},{16,32},{24,40},{32,48},{40,56},{48,64},{56,72},{64,... | collective-permute-start | bytes 786440 | tf_op jit(solution)/shard_map/ppermute | solution.py:266
  4.1 1.0 %copy-start = (bf16[32,8192]{1,0:T(8,128)(2,1)S(1)}, bf16[32,8192]{1,0:T(8,128)(2,1)}, u32[]{:S(2)}) copy-start(bf16[32,8192]{1,0:T(8,128)(2,1)} %queries.1) | copy-start | bytes 1572868
  6.0 22.6 %all-to-all-start = ((bf16[8,32,1024]{2,1,0:T(8,128)(2,1)}), bf16[8,32,1024]{2,1,0:T(8,128)(2,1)S(1)}, u32[]{:S(2)}, u32[]{:S(2)}) async-start(bf16[8,32,1024]{2,1,0:T(8,128)(2,1)} %cut.1), calls=%async_computation | async-start | bytes 1048576 | tf_op jit(solution)/shard_map/all_to_all | solution.py:269
  13.7 4.1 %copy-start.1 = (bf16[2,2048,128]{2,1,0:T(8,128)(2,1)S(1)}, bf16[2,2048,128]{2,1,0:T(8,128)(2,1)}, u32[]{:S(2)}) copy-start(bf16[2,2048,128]{2,1,0:T(8,128)(2,1)} %part_ref.1) | copy-start | bytes 3145732
  14.3 8.5 %collective-permute-start.1 = (bf16[2,512,128]{2,1,0:T(8,128)(2,1)S(1)}, bf16[2,512,128]{2,1,0:T(8,128)(2,1)S(1)}, u32[]{:S(2)}, u32[]{:S(2)}) collective-permute-start(bf16[2,512,128]{2,1,0:T(8,128)(2,1)S(1)} %choose.2.after.held), channel_id=1, source_target_pairs={{0,32},{8,40},{16,48},{24,56},{32,64},{40,72},{48,80},{56,88},{64,... | collective-permute-start | bytes 786440 | tf_op jit(solution)/shard_map/ppermute | solution.py:266
  23.3 10.7 %collective-permute-start.2 = (bf16[2,512,128]{2,1,0:T(8,128)(2,1)S(1)}, bf16[2,512,128]{2,1,0:T(8,128)(2,1)S(1)}, u32[]{:S(2)}, u32[]{:S(2)}) collective-permute-start(bf16[2,512,128]{2,1,0:T(8,128)(2,1)S(1)} %choose.3.held), channel_id=1, source_target_pairs={{0,8},{8,16},{16,24},{24,32},{32,40},{40,48},{48,56},{56,64},{64,7... | collective-permute-start | bytes 786440 | tf_op jit(solution)/shard_map/ppermute | solution.py:266

commit v4 on v3

--- a/solution.py
+++ b/solution.py
@@ -35,8 +35,16 @@
         outgoing[h] = queries[:, h * width:(h + 1) * width]
 
 
-def choose_kernel(shift, scalars, moved, held, after, out):
-    arrived = (scalars[1] & shift) != 0
+def full_tiles_of(facts):
+    return jnp.max(facts[0])
+
+
+def place_of(facts):
+    return jnp.max(facts[1])
+
+
+def choose_kernel(shift, facts, moved, held, after, out):
+    arrived = (place_of(facts) & shift) != 0
 
     @pl.when(arrived)
     def _():
@@ -83,9 +91,9 @@
     return col - row
 
 
-def local_kernel(scalars, q_ref, keys, vals, state_ref, weights):
+def local_kernel(facts, q_ref, keys, vals, state_ref, weights):
     stacks = state_ref.shape[0] // STACK
-    full_tiles = scalars[0]
+    full_tiles = full_tiles_of(facts)
     slant = causal_slant()
 
     def attend(chunks):
@@ -139,11 +147,11 @@
     return lax.fori_loop(0, base, functools.partial(mix_from, 0, anchor[1]), mixed)
 
 
-def anchor_kernel(scalars, moved, held, q_ref, local_keys, local_vals, states, out_ref,
+def anchor_kernel(facts, moved, held, q_ref, local_keys, local_vals, states, out_ref,
                   anchor, keys, vals, weights, scores):
     heads = states.shape[0]
-    has_anchor = scalars[1] > 0
-    choose_kernel(1, scalars, moved, held, None, anchor)
+    has_anchor = place_of(facts) > 0
+    choose_kernel(1, facts, moved, held, None, anchor)
     widen_into(anchor, keys, vals)
 
     def write(g, mixed):
@@ -167,7 +175,7 @@
     @pl.when(jnp.logical_not(safe))
     def _():
         for g in range(heads):
-            write(g, exact_head(g, scalars[0], has_anchor, q_ref, (local_keys, local_vals), (keys, vals), scores))
+            write(g, exact_head(g, full_tiles_of(facts), has_anchor, q_ref, (local_keys, local_vals), (keys, vals), scores))
 
 
 def cost(heads, keys):
@@ -201,16 +209,16 @@
     )(queries, after)
 
 
-def choose(shift, scalars, moved, held, after, estimate):
+def choose(shift, facts, moved, held, after, estimate):
     return pl.pallas_call(
         functools.partial(choose_kernel, shift),
         out_shape=jax.ShapeDtypeStruct(held.shape, held.dtype),
-        in_specs=[smem, vmem, vmem, anywhere],
+        in_specs=[vmem, vmem, vmem, anywhere],
         out_specs=vmem,
         compiler_params=small,
         cost_estimate=estimate,
         name="choose",
-    )(scalars, moved, held, after)
+    )(facts, moved, held, after)
 
 
 def widen(kv, after):
@@ -225,24 +233,24 @@
     )(kv, after)
 
 
-def attend_local(scalars, q, keys, vals):
+def attend_local(facts, q, keys, vals):
     return pl.pallas_call(
         local_kernel,
         out_shape=jax.ShapeDtypeStruct((GROUP, BLOCK_QUERIES, 2 * HEAD_SIZE), jnp.float32),
-        in_specs=[smem, vmem, vmem, vmem],
+        in_specs=[vmem] * 4,
         out_specs=vmem,
         scratch_shapes=[pltpu.VMEM((2, STACK * BLOCK_QUERIES, CACHE_SLOTS), jnp.bfloat16)],
         compiler_params=params,
         cost_estimate=cost(GROUP, CACHE_SLOTS),
         name="attend_local",
-    )(scalars, q, keys, vals)
-
-
-def attend_anchor(scalars, moved, held, q, keys, vals, states):
+    )(facts, q, keys, vals)
+
+
+def attend_anchor(facts, moved, held, q, keys, vals, states):
     return pl.pallas_call(
         anchor_kernel,
         out_shape=jax.ShapeDtypeStruct(q.shape, jnp.bfloat16),
-        in_specs=[smem] + [vmem] * 6,
+        in_specs=[vmem] * 7,
         out_specs=vmem,
         scratch_shapes=[
             pltpu.VMEM(held.shape, held.dtype),
@@ -253,13 +261,14 @@
         compiler_params=params,
         cost_estimate=cost(GROUP, ANCHOR_SLOTS),
         name="attend_anchor",
-    )(scalars, moved, held, q, keys, vals, states)
+    )(facts, moved, held, q, keys, vals, states)
 
 
 def body(queries, kv_cache, anchor_src, stretch_pos):
     block = lax.axis_index("ctx").astype(jnp.int32)
     blocks = lax.axis_size("ctx")
-    scalars = jnp.stack([stretch_pos[0] // TILE, block - anchor_src[0]])
+    which = lax.broadcasted_iota(jnp.int32, (2, 8, 128), 0)
+    facts = jnp.where(which == 0, stretch_pos.reshape(1, 1, 1) // TILE, block - anchor_src.reshape(1, 1, 1))
     held = lax.optimization_barrier(kv_cache[:, :ANCHOR_SLOTS, :])
 
     def from_earlier(held, shift):
@@ -268,13 +277,13 @@
     moved = from_earlier(held, 2)
     q = lax.all_to_all(cut(queries, held), "head", split_axis=0, concat_axis=0, tiled=True)
     q = q.reshape(BLOCK_QUERIES, GROUP * HEAD_SIZE)
-    held = choose(2, scalars, moved, held, scalars, cost(GROUP, CACHE_SLOTS))
+    held = choose(2, facts, moved, held, facts, cost(GROUP, CACHE_SLOTS))
     moved = from_earlier(held, 4)
     keys, vals = widen(kv_cache, held)
-    held = choose(4, scalars, moved, held, keys, slight)
+    held = choose(4, facts, moved, held, keys, slight)
     moved = from_earlier(held, 1)
-    states = attend_local(scalars, q, keys, vals)
-    result = attend_anchor(scalars, moved, held, q, keys, vals, states)
+    states = attend_local(facts, q, keys, vals)
+    result = attend_anchor(facts, moved, held, q, keys, vals, states)
     return lax.all_to_all(result, "head", split_axis=0, concat_axis=1, tiled=True)
 
 

time: 94.4 us -> 94.4 us (level)
  the two profiles are of different devices: /device:TPU:33 before, /device:TPU:160 now
where the time goes in v4:
time: 94.4 us; the launch traced here: 94.1 us
  Pallas kernels  47.8 us (51%)
  blocking collectives  19.2 us (20%)
  starting transfers between devices  15.9 us (17%)
  waiting for transfers between devices  6.87 us (7%)
  local copies, waits for them, and re-layouts  2.91 us (3%)
  between operations  1.43 us (2%)
    pallas_call x1, Pallas kernels, attend_anchor(): pl.pallas_call(anchor_kernel, out_shape=jax.ShapeDtypeStruct(q.shape, jnp...  41.2 us
    all_to_all x1, blocking collectives, body(): lax.all_to_all(result, 'head', split_axis=0, concat_axis=1, tiled=True)  19.2 us
    ppermute x3, starting transfers between devices, from_earlier(): lax.ppermute(held, 'ctx', [(b, b + shift) for b in range(blocks - shift)])  9.28 us
    ppermute x3, waiting for transfers between devices, from_earlier(): lax.ppermute(held, 'ctx', [(b, b + shift) for b in range(blocks - shift)])  6.86 us
    all_to_all x1, starting transfers between devices, body(): lax.all_to_all(cut(queries, held), 'head', split_axis=0, concat_axis=0, t...  6.64 us
    pallas_call x1, Pallas kernels, attend_local(): pl.pallas_call(local_kernel, out_shape=jax.ShapeDtypeStruct((GROUP, BLOCK...  5.02 us
  transfers between devices with their start and end apart: 4, of which 2 were waited for; matrix products, arithmetic and copies ran while one was open for 0% of the time, Pallas kernels for 7%

profile of v4, /device:TPU:160, one launch (start us, length us, event | category | flops | bytes accessed | tf_op | source)
XLA Modules:
  0.0 94.1 jit_solution(14960035869601884879)
XLA Ops:
  0.0 1.0 %slice.3.held.after = bf16[2,512,128]{2,1,0:T(8,128)(2,1)S(1)} slice(bf16[2,2048,128]{2,1,0:T(8,128)(2,1)} %part_ref.1), slice={[0:2], [0:512], [0:128]} | slice | bytes 524288 | tf_op jit(solution)/shard_map/slice | solution.py:272
  1.0 3.4 %collective-permute-start = (bf16[2,512,128]{2,1,0:T(8,128)(2,1)S(1)}, bf16[2,512,128]{2,1,0:T(8,128)(2,1)S(1)}, u32[]{:S(2)}, u32[]{:S(2)}) collective-permute-start(bf16[2,512,128]{2,1,0:T(8,128)(2,1)S(1)} %slice.3.held.after), channel_id=1, source_target_pairs={{0,16},{8,24},{16,32},{24,40},{32,48},{40,56},{48,64},{56,72},{64,... | collective-permute-start | bytes 786440 | tf_op jit(solution)/shard_map/ppermute | solution.py:275
  4.4 0.0 copy-start
  4.4 1.0 %copy-done = bf16[32,8192]{1,0:T(8,128)(2,1)S(1)} copy-done((bf16[32,8192]{1,0:T(8,128)(2,1)S(1)}, bf16[32,8192]{1,0:T(8,128)(2,1)}, u32[]{:S(2)}) %copy-start) | copy-done | bytes 524312
  5.4 0.8 cut.1
  6.3 6.6 %all-to-all-start = ((bf16[8,32,1024]{2,1,0:T(8,128)(2,1)}), bf16[8,32,1024]{2,1,0:T(8,128)(2,1)S(1)}, u32[]{:S(2)}, u32[]{:S(2)}) async-start(bf16[8,32,1024]{2,1,0:T(8,128)(2,1)} %cut.1), calls=%async_computation | async-start | bytes 1048576 | tf_op jit(solution)/shard_map/all_to_all | solution.py:278
  14.2 0.0 collective-permute-done.moved
  14.2 0.1 iota.7.facts.after
  14.3 0.0 copy-start.1
  14.3 0.2 choose.2.after.held
  14.5 4.0 %collective-permute-start.1 = (bf16[2,512,128]{2,1,0:T(8,128)(2,1)S(1)}, bf16[2,512,128]{2,1,0:T(8,128)(2,1)S(1)}, u32[]{:S(2)}, u32[]{:S(2)}) collective-permute-start(bf16[2,512,128]{2,1,0:T(8,128)(2,1)S(1)} %choose.2.after.held), channel_id=1, source_target_pairs={{0,32},{8,40},{16,48},{24,56},{32,64},{40,72},{48,80},{56,88},{64,... | collective-permute-start | bytes 786440 | tf_op jit(solution)/shard_map/ppermute | solution.py:275
  18.5 0.0 copy-done.1
  18.5 0.3 widen.1
  18.8 5.2 %collective-permute-done.1.moved = bf16[2,512,128]{2,1,0:T(8,128)(2,1)S(1)} collective-permute-done((bf16[2,512,128]{2,1,0:T(8,128)(2,1)S(1)}, bf16[2,512,128]{2,1,0:T(8,128)(2,1)S(1)}, u32[]{:S(2)}, u32[]{:S(2)}) %collective-permute-start.1) | collective-permute-done | bytes 262176 | tf_op jit(solution)/shard_map/ppermute | solution.py:275
  24.0 0.2 choose.3.held
  24.3 1.9 %collective-permute-start.2 = (bf16[2,512,128]{2,1,0:T(8,128)(2,1)S(1)}, bf16[2,512,128]{2,1,0:T(8,128)(2,1)S(1)}, u32[]{:S(2)}, u32[]{:S(2)}) collective-permute-start(bf16[2,512,128]{2,1,0:T(8,128)(2,1)S(1)} %choose.3.held), channel_id=1, source_target_pairs={{0,8},{8,16},{16,24},{24,32},{32,40},{40,48},{48,56},{56,64},{64,7... | collective-permute-start | bytes 786440 | tf_op jit(solution)/shard_map/ppermute | solution.py:275
  26.2 0.0 all-to-all-done
  26.2 5.0 %attend_local.1.states = f32[8,256,256]{2,1,0:T(8,128)S(1)} custom-call(s32[2,8,128]{2,1,0:T(8,128)S(1)} %iota.7.facts.after, bf16[256,1024]{1,0:T(8,128)(2,1)S(1)} %bitcast.15, bf16[128,2048]{1,0:T(8,128)(2,1)S(1)} %get-tuple-element.7.after.keys.local_keys, bf16[2048,256]{1,0:T(8,128)(2,1)S(1)} %get-tuple-element.8.vals.local_vals), custom_call_target="tpu_custom_call" | custom-call | flops 2147483648 | bytes 2097152 | tf_op jit(solution)/shard_map/attend_local/pallas_call | solution.py:237
  31.2 1.6 %collective-permute-done.2.moved = bf16[2,512,128]{2,1,0:T(8,128)(2,1)S(1)} collective-permute-done((bf16[2,512,128]{2,1,0:T(8,128)(2,1)S(1)}, bf16[2,512,128]{2,1,0:T(8,128)(2,1)S(1)}, u32[]{:S(2)}, u32[]{:S(2)}) %collective-permute-start.2) | collective-permute-done | bytes 262176 | tf_op jit(solution)/shard_map/ppermute | solution.py:275
  32.9 41.2 %attend_anchor.1 = bf16[256,1024]{1,0:T(8,128)(2,1)S(1)} custom-call(s32[2,8,128]{2,1,0:T(8,128)S(1)} %iota.7.facts.after, bf16[2,512,128]{2,1,0:T(8,128)(2,1)S(1)} %collective-permute-done.2.moved, bf16[2,512,128]{2,1,0:T(8,128)(2,1)S(1)} %choose.3.held, bf16[256,1024]{1,0:T(8,128)(2,1)S(1)} %bitcast.16, ...), custom_call_target="tpu_custom_call" | custom-call | flops 536870912 | bytes 2097152 | tf_op jit(solution)/shard_map/attend_anchor/pallas_call | solution.py:250
  74.0 19.2 %all_to_all.24 = bf16[8,32,1024]{2,1,0:T(8,128)(2,1)S(1)} all-to-all(bf16[8,32,1024]{2,1,0:T(8,128)(2,1)S(1)} %bitcast.17), channel_id=1, replica_groups=mesh['ctx'=64,'head'=8] {'head'}, dimensions={0} | all-to-all | bytes 1048576 | tf_op jit(solution)/shard_map/all_to_all | solution.py:287
  93.2 0.8 copy.6
  (1 shorter events, 0.0 us)
Async XLA Ops:
  1.0 13.3 %collective-permute-start = (bf16[2,512,128]{2,1,0:T(8,128)(2,1)S(1)}, bf16[2,512,128]{2,1,0:T(8,128)(2,1)S(1)}, u32[]{:S(2)}, u32[]{:S(2)}) collective-permute-start(bf16[2,512,128]{2,1,0:T(8,128)(2,1)S(1)} %slice.3.held.after), channel_id=1, source_target_pairs={{0,16},{8,24},{16,32},{24,40},{32,48},{40,56},{48,64},{56,72},{64,... | collective-permute-start | bytes 786440 | tf_op jit(solution)/shard_map/ppermute | solution.py:275
  4.4 1.0 %copy-start = (bf16[32,8192]{1,0:T(8,128)(2,1)S(1)}, bf16[32,8192]{1,0:T(8,128)(2,1)}, u32[]{:S(2)}) copy-start(bf16[32,8192]{1,0:T(8,128)(2,1)} %queries.1) | copy-start | bytes 1572868
  6.3 20.0 %all-to-all-start = ((bf16[8,32,1024]{2,1,0:T(8,128)(2,1)}), bf16[8,32,1024]{2,1,0:T(8,128)(2,1)S(1)}, u32[]{:S(2)}, u32[]{:S(2)}) async-start(bf16[8,32,1024]{2,1,0:T(8,128)(2,1)} %cut.1), calls=%async_computation | async-start | bytes 1048576 | tf_op jit(solution)/shard_map/all_to_all | solution.py:278
  14.3 4.2 %copy-start.1 = (bf16[2,2048,128]{2,1,0:T(8,128)(2,1)S(1)}, bf16[2,2048,128]{2,1,0:T(8,128)(2,1)}, u32[]{:S(2)}) copy-start(bf16[2,2048,128]{2,1,0:T(8,128)(2,1)} %part_ref.1) | copy-start | bytes 3145732
  14.5 9.5 %collective-permute-start.1 = (bf16[2,512,128]{2,1,0:T(8,128)(2,1)S(1)}, bf16[2,512,128]{2,1,0:T(8,128)(2,1)S(1)}, u32[]{:S(2)}, u32[]{:S(2)}) collective-permute-start(bf16[2,512,128]{2,1,0:T(8,128)(2,1)S(1)} %choose.2.after.held), channel_id=1, source_target_pairs={{0,32},{8,40},{16,48},{24,56},{32,64},{40,72},{48,80},{56,88},{64,... | collective-permute-start | bytes 786440 | tf_op jit(solution)/shard_map/ppermute | solution.py:275
  24.3 8.6 %collective-permute-start.2 = (bf16[2,512,128]{2,1,0:T(8,128)(2,1)S(1)}, bf16[2,512,128]{2,1,0:T(8,128)(2,1)S(1)}, u32[]{:S(2)}, u32[]{:S(2)}) collective-permute-start(bf16[2,512,128]{2,1,0:T(8,128)(2,1)S(1)} %choose.3.held), channel_id=1, source_target_pairs={{0,8},{8,16},{16,24},{24,32},{32,40},{40,48},{48,56},{56,64},{64,7... | collective-permute-start | bytes 786440 | tf_op jit(solution)/shard_map/ppermute | solution.py:275

commit v5 on v4

--- a/solution.py
+++ b/solution.py
@@ -17,6 +17,7 @@
 ANCHOR_SLOTS = 512
 SPAN = 8
 TILE = 256
+FIRST_HEADS = 4
 STACK = 2
 CHUNK = 512
 
@@ -69,8 +70,8 @@
     return jnp.dot(q, keys, preferred_element_type=jnp.float32) * EXP2_SCALE
 
 
-def stacked(q_ref, stack):
-    return jnp.concatenate([q_ref[:, head_columns(stack * STACK + g)] for g in range(STACK)], axis=0)
+def stacked(q_ref, first):
+    return jnp.concatenate([q_ref[:, head_columns(first + g)] for g in range(STACK)], axis=0)
 
 
 def rows_of(g):
@@ -91,7 +92,7 @@
     return col - row
 
 
-def local_kernel(facts, q_ref, keys, vals, state_ref, weights):
+def local_kernel(first, facts, q_ref, keys, vals, state_ref, weights):
     stacks = state_ref.shape[0] // STACK
     full_tiles = full_tiles_of(facts)
     slant = causal_slant()
@@ -101,7 +102,7 @@
         tiles = span // TILE
 
         def weigh(stack):
-            q = stacked(q_ref, stack)
+            q = stacked(q_ref, first + stack * STACK)
             for tile in range(tiles):
                 s = scaled_scores(q, keys[:, tile_of(tile)])
                 if tile * TILE >= span - CHUNK:
@@ -147,9 +148,10 @@
     return lax.fori_loop(0, base, functools.partial(mix_from, 0, anchor[1]), mixed)
 
 
-def anchor_kernel(facts, moved, held, q_ref, local_keys, local_vals, states, out_ref,
+def anchor_kernel(facts, moved, held, q_ref, local_keys, local_vals, early, late, out_ref,
                   anchor, keys, vals, weights, scores):
-    heads = states.shape[0]
+    states = [part.at[g] for part in (early, late) for g in range(part.shape[0])]
+    heads = len(states)
     has_anchor = place_of(facts) > 0
     choose_kernel(1, facts, moved, held, None, anchor)
     widen_into(anchor, keys, vals)
@@ -158,13 +160,13 @@
         out_ref[:, head_columns(g)] = (mixed[:, :HEAD_SIZE] / mixed[:, HEAD_SIZE:]).astype(jnp.bfloat16)
 
     for stack in range(heads // STACK):
-        s = jnp.where(has_anchor, scaled_scores(stacked(q_ref, stack), keys[...]), masked_score)
+        s = jnp.where(has_anchor, scaled_scores(stacked(q_ref, stack * STACK), keys[...]), masked_score)
         weights[stack] = jnp.exp2(s).astype(jnp.bfloat16)
     low = high = None
     for stack in range(heads // STACK):
         both = jnp.dot(weights[stack], vals[...], preferred_element_type=jnp.float32)
         for g in range(STACK):
-            state = states[stack * STACK + g]
+            state = states[stack * STACK + g][...]
             mixed = both[rows_of(g)] + state
             write(stack * STACK + g, mixed)
             below, above = state[:, HEAD_SIZE:], mixed[:, HEAD_SIZE:]
@@ -233,10 +235,10 @@
     )(kv, after)
 
 
-def attend_local(facts, q, keys, vals):
-    return pl.pallas_call(
-        local_kernel,
-        out_shape=jax.ShapeDtypeStruct((GROUP, BLOCK_QUERIES, 2 * HEAD_SIZE), jnp.float32),
+def attend_local(first, heads, facts, q, keys, vals):
+    return pl.pallas_call(
+        functools.partial(local_kernel, first),
+        out_shape=jax.ShapeDtypeStruct((heads, BLOCK_QUERIES, 2 * HEAD_SIZE), jnp.float32),
         in_specs=[vmem] * 4,
         out_specs=vmem,
         scratch_shapes=[pltpu.VMEM((2, STACK * BLOCK_QUERIES, CACHE_SLOTS), jnp.bfloat16)],
@@ -246,11 +248,11 @@
     )(facts, q, keys, vals)
 
 
-def attend_anchor(facts, moved, held, q, keys, vals, states):
+def attend_anchor(facts, moved, held, q, keys, vals, early, late):
     return pl.pallas_call(
         anchor_kernel,
         out_shape=jax.ShapeDtypeStruct(q.shape, jnp.bfloat16),
-        in_specs=[vmem] * 7,
+        in_specs=[vmem] * 8,
         out_specs=vmem,
         scratch_shapes=[
             pltpu.VMEM(held.shape, held.dtype),
@@ -261,7 +263,7 @@
         compiler_params=params,
         cost_estimate=cost(GROUP, ANCHOR_SLOTS),
         name="attend_anchor",
-    )(facts, moved, held, q, keys, vals, states)
+    )(facts, moved, held, q, keys, vals, early, late)
 
 
 def body(queries, kv_cache, anchor_src, stretch_pos):
@@ -281,9 +283,11 @@
     moved = from_earlier(held, 4)
     keys, vals = widen(kv_cache, held)
     held = choose(4, facts, moved, held, keys, slight)
+    early = attend_local(0, FIRST_HEADS, facts, q, keys, vals)
+    held, early = lax.optimization_barrier((held, early))
     moved = from_earlier(held, 1)
-    states = attend_local(facts, q, keys, vals)
-    result = attend_anchor(facts, moved, held, q, keys, vals, states)
+    late = attend_local(FIRST_HEADS, GROUP - FIRST_HEADS, facts, q, keys, vals)
+    result = attend_anchor(facts, moved, held, q, keys, vals, early, late)
     return lax.all_to_all(result, "head", split_axis=0, concat_axis=1, tiled=True)
 
 

time: 94.4 us -> 92 us (0.975)
  the two profiles are of different devices: /device:TPU:160 before, /device:TPU:96 now
where the time goes in v5:
time: 92 us; the launch traced here: 91.7 us
  Pallas kernels  48.1 us (52%)
  starting transfers between devices  17.1 us (19%)
  blocking collectives  14.8 us (16%)
  waiting for transfers between devices  8.26 us (9%)
  local copies, waits for them, and re-layouts  1.94 us (2%)
  between operations  1.43 us (2%)
    pallas_call x1, Pallas kernels, attend_anchor(): pl.pallas_call(anchor_kernel, out_shape=jax.ShapeDtypeStruct(q.shape, jnp...  41.4 us
    all_to_all x1, blocking collectives, body(): lax.all_to_all(result, 'head', split_axis=0, concat_axis=1, tiled=True)  14.8 us
    ppermute x3, starting transfers between devices, from_earlier(): lax.ppermute(held, 'ctx', [(b, b + shift) for b in range(blocks - shift)])  10.5 us
    all_to_all x1, starting transfers between devices, body(): lax.all_to_all(cut(queries, held), 'head', split_axis=0, concat_axis=0, t...  6.64 us
    pallas_call x2, Pallas kernels, attend_local(): pl.pallas_call(functools.partial(local_kernel, first), out_shape=jax.Shap...  5.15 us
    all_to_all x1, waiting for transfers between devices, body(): lax.all_to_all(cut(queries, held), 'head', split_axis=0, concat_axis=0, t...  4.17 us
    ppermute x3, waiting for transfers between devices, from_earlier(): lax.ppermute(held, 'ctx', [(b, b + shift) for b in range(blocks - shift)])  4.09 us
  transfers between devices with their start and end apart: 4, of which 2 were waited for; matrix products, arithmetic and copies ran while one was open for 0% of the time, Pallas kernels for 7%

profile of v5, /device:TPU:96, one launch (start us, length us, event | category | flops | bytes accessed | tf_op | source)
XLA Modules:
  0.0 91.7 jit_solution(4535034181389693394)
XLA Ops:
  0.0 0.0 copy-start
  0.0 1.0 %slice.3.held.after = bf16[2,512,128]{2,1,0:T(8,128)(2,1)S(1)} slice(bf16[2,2048,128]{2,1,0:T(8,128)(2,1)} %part_ref.1), slice={[0:2], [0:512], [0:128]} | slice | bytes 524288 | tf_op jit(solution)/shard_map/slice | solution.py:274
  1.0 3.4 %collective-permute-start = (bf16[2,512,128]{2,1,0:T(8,128)(2,1)S(1)}, bf16[2,512,128]{2,1,0:T(8,128)(2,1)S(1)}, u32[]{:S(2)}, u32[]{:S(2)}) collective-permute-start(bf16[2,512,128]{2,1,0:T(8,128)(2,1)S(1)} %slice.3.held.after), channel_id=1, source_target_pairs={{0,16},{8,24},{16,32},{24,40},{32,48},{40,56},{48,64},{56,72},{64,... | collective-permute-start | bytes 786440 | tf_op jit(solution)/shard_map/ppermute | solution.py:277
  4.4 0.0 copy-done
  4.4 0.8 cut.1
  5.3 6.6 %all-to-all-start = ((bf16[8,32,1024]{2,1,0:T(8,128)(2,1)}), bf16[8,32,1024]{2,1,0:T(8,128)(2,1)S(1)}, u32[]{:S(2)}, u32[]{:S(2)}) async-start(bf16[8,32,1024]{2,1,0:T(8,128)(2,1)} %cut.1), calls=%async_computation | async-start | bytes 1048576 | tf_op jit(solution)/shard_map/all_to_all | solution.py:280
  13.2 0.0 collective-permute-done.moved
  13.3 0.1 iota.7.facts.after
  13.3 0.0 copy-start.1
  13.3 0.2 choose.2.after.held
  13.6 5.2 %collective-permute-start.1 = (bf16[2,512,128]{2,1,0:T(8,128)(2,1)S(1)}, bf16[2,512,128]{2,1,0:T(8,128)(2,1)S(1)}, u32[]{:S(2)}, u32[]{:S(2)}) collective-permute-start(bf16[2,512,128]{2,1,0:T(8,128)(2,1)S(1)} %choose.2.after.held), channel_id=1, source_target_pairs={{0,32},{8,40},{16,48},{24,56},{32,64},{40,72},{48,80},{56,88},{64,... | collective-permute-start | bytes 786440 | tf_op jit(solution)/shard_map/ppermute | solution.py:277
  18.7 0.0 copy-done.1
  18.7 0.3 widen.1
  19.0 4.2 %all-to-all-done = bf16[8,32,1024]{2,1,0:T(8,128)(2,1)S(1)} async-done(((bf16[8,32,1024]{2,1,0:T(8,128)(2,1)}), bf16[8,32,1024]{2,1,0:T(8,128)(2,1)S(1)}, u32[]{:S(2)}, u32[]{:S(2)}) %all-to-all-start) | async-done | bytes 524320 | tf_op jit(solution)/shard_map/all_to_all | solution.py:280
  23.2 2.6 %attend_local.2.early = f32[4,256,256]{2,1,0:T(8,128)S(1)} custom-call(s32[2,8,128]{2,1,0:T(8,128)S(1)} %iota.7.facts.after, bf16[256,1024]{1,0:T(8,128)(2,1)S(1)} %bitcast.15, bf16[128,2048]{1,0:T(8,128)(2,1)S(1)} %get-tuple-element.9.after.keys.local_keys, bf16[2048,256]{1,0:T(8,128)(2,1)S(1)} %get-tuple-element.10.vals.local_vals), custom_call_target="tpu_custom_call" | custom-call | flops 2147483648 | bytes 2097152 | tf_op jit(solution)/shard_map/attend_local/pallas_call | solution.py:239
  25.8 0.0 collective-permute-done.1.moved
  25.8 0.2 choose.3.held
  26.0 1.9 %collective-permute-start.2 = (bf16[2,512,128]{2,1,0:T(8,128)(2,1)S(1)}, bf16[2,512,128]{2,1,0:T(8,128)(2,1)S(1)}, u32[]{:S(2)}, u32[]{:S(2)}) collective-permute-start(bf16[2,512,128]{2,1,0:T(8,128)(2,1)S(1)} %choose.3.held), channel_id=1, source_target_pairs={{0,8},{8,16},{16,24},{24,32},{32,40},{40,48},{48,56},{56,64},{64,7... | collective-permute-start | bytes 786440 | tf_op jit(solution)/shard_map/ppermute | solution.py:277
  28.0 2.6 %attend_local.3.late = f32[4,256,256]{2,1,0:T(8,128)S(1)} custom-call(s32[2,8,128]{2,1,0:T(8,128)S(1)} %iota.7.facts.after, bf16[256,1024]{1,0:T(8,128)(2,1)S(1)} %bitcast.16, bf16[128,2048]{1,0:T(8,128)(2,1)S(1)} %get-tuple-element.9.after.keys.local_keys, bf16[2048,256]{1,0:T(8,128)(2,1)S(1)} %get-tuple-element.10.vals.local_vals), custom_call_target="tpu_custom_call" | custom-call | flops 2147483648 | bytes 2097152 | tf_op jit(solution)/shard_map/attend_local/pallas_call | solution.py:239
  30.5 4.1 %collective-permute-done.2.moved = bf16[2,512,128]{2,1,0:T(8,128)(2,1)S(1)} collective-permute-done((bf16[2,512,128]{2,1,0:T(8,128)(2,1)S(1)}, bf16[2,512,128]{2,1,0:T(8,128)(2,1)S(1)}, u32[]{:S(2)}, u32[]{:S(2)}) %collective-permute-start.2) | collective-permute-done | bytes 262176 | tf_op jit(solution)/shard_map/ppermute | solution.py:277
  34.6 41.4 %attend_anchor.1 = bf16[256,1024]{1,0:T(8,128)(2,1)S(1)} custom-call(s32[2,8,128]{2,1,0:T(8,128)S(1)} %iota.7.facts.after, bf16[2,512,128]{2,1,0:T(8,128)(2,1)S(1)} %collective-permute-done.2.moved, bf16[2,512,128]{2,1,0:T(8,128)(2,1)S(1)} %choose.3.held, bf16[256,1024]{1,0:T(8,128)(2,1)S(1)} %bitcast.17, ...), custom_call_target="tpu_custom_call" | custom-call | flops 536870912 | bytes 2097152 | tf_op jit(solution)/shard_map/attend_anchor/pallas_call | solution.py:252
  76.0 14.8 %all_to_all.24 = bf16[8,32,1024]{2,1,0:T(8,128)(2,1)S(1)} all-to-all(bf16[8,32,1024]{2,1,0:T(8,128)(2,1)S(1)} %bitcast.18), channel_id=1, replica_groups=mesh['ctx'=64,'head'=8] {'head'}, dimensions={0} | all-to-all | bytes 1048576 | tf_op jit(solution)/shard_map/all_to_all | solution.py:291
  90.8 0.8 copy.6
  (1 shorter events, 0.0 us)
Async XLA Ops:
  0.0 4.4 %copy-start = (bf16[32,8192]{1,0:T(8,128)(2,1)S(1)}, bf16[32,8192]{1,0:T(8,128)(2,1)}, u32[]{:S(2)}) copy-start(bf16[32,8192]{1,0:T(8,128)(2,1)} %queries.1) | copy-start | bytes 1572868
  1.0 12.2 %collective-permute-start = (bf16[2,512,128]{2,1,0:T(8,128)(2,1)S(1)}, bf16[2,512,128]{2,1,0:T(8,128)(2,1)S(1)}, u32[]{:S(2)}, u32[]{:S(2)}) collective-permute-start(bf16[2,512,128]{2,1,0:T(8,128)(2,1)S(1)} %slice.3.held.after), channel_id=1, source_target_pairs={{0,16},{8,24},{16,32},{24,40},{32,48},{40,56},{48,64},{56,72},{64,... | collective-permute-start | bytes 786440 | tf_op jit(solution)/shard_map/ppermute | solution.py:277
  5.3 17.9 %all-to-all-start = ((bf16[8,32,1024]{2,1,0:T(8,128)(2,1)}), bf16[8,32,1024]{2,1,0:T(8,128)(2,1)S(1)}, u32[]{:S(2)}, u32[]{:S(2)}) async-start(bf16[8,32,1024]{2,1,0:T(8,128)(2,1)} %cut.1), calls=%async_computation | async-start | bytes 1048576 | tf_op jit(solution)/shard_map/all_to_all | solution.py:280
  13.3 5.4 %copy-start.1 = (bf16[2,2048,128]{2,1,0:T(8,128)(2,1)S(1)}, bf16[2,2048,128]{2,1,0:T(8,128)(2,1)}, u32[]{:S(2)}) copy-start(bf16[2,2048,128]{2,1,0:T(8,128)(2,1)} %part_ref.1) | copy-start | bytes 3145732
  13.6 12.2 %collective-permute-start.1 = (bf16[2,512,128]{2,1,0:T(8,128)(2,1)S(1)}, bf16[2,512,128]{2,1,0:T(8,128)(2,1)S(1)}, u32[]{:S(2)}, u32[]{:S(2)}) collective-permute-start(bf16[2,512,128]{2,1,0:T(8,128)(2,1)S(1)} %choose.2.after.held), channel_id=1, source_target_pairs={{0,32},{8,40},{16,48},{24,56},{32,64},{40,72},{48,80},{56,88},{64,... | collective-permute-start | bytes 786440 | tf_op jit(solution)/shard_map/ppermute | solution.py:277
  26.0 8.6 %collective-permute-start.2 = (bf16[2,512,128]{2,1,0:T(8,128)(2,1)S(1)}, bf16[2,512,128]{2,1,0:T(8,128)(2,1)S(1)}, u32[]{:S(2)}, u32[]{:S(2)}) collective-permute-start(bf16[2,512,128]{2,1,0:T(8,128)(2,1)S(1)} %choose.3.held), channel_id=1, source_target_pairs={{0,8},{8,16},{16,24},{24,32},{32,40},{40,48},{48,56},{56,64},{64,7... | collective-permute-start | bytes 786440 | tf_op jit(solution)/shard_map/ppermute | solution.py:277
